TPU v7x, 512 devices: a whole 4x8x8 slice. The times are simulated.
512 devices in a mesh: seq: 32 (over x, z), chan: 16 (over y, core).
Axes of the slice: x: 4, y: 8, z: 8, core: 2. Of those that a mesh axis runs over, the one named last changes fastest.
Arguments:
- query_feat: bfloat16 [16384, 8192], P('seq', 'chan'), may hold values from -6 to 6
- key_feat: bfloat16 [16384, 8192], P('seq', 'chan'), may hold values from -6 to 6
- value_feat: bfloat16 [16384, 8192], P('seq', 'chan'), may hold values from -6 to 6
- decay_rate: float32 [8, 8192], P(None, 'chan'), may hold values from 1e-05 to 0.05
- residues: float32 [8, 8192], P(None, 'chan'), may hold values from -4 to 4
- skip_gain: float32 [8192], P('chan'), may hold values from -1 to 1
- norm_gain: float32 [8192], P('chan'), may hold values from 0.25 to 1.75
- doc_starts: int32 [256], replicated, may hold values from 0 to 1, as said below
- cotangent: bfloat16 [16384, 8192], P('seq', 'chan'), may hold values from -6 to 6
Outputs:
- mixed: bfloat16 [16384, 8192], P('seq', 'chan')
- grad_query: bfloat16 [16384, 8192], P('seq', 'chan')
- grad_key: bfloat16 [16384, 8192], P('seq', 'chan')
- grad_value: bfloat16 [16384, 8192], P('seq', 'chan')
Inputs may be any that keep to these rules, and one draw needn't show every extreme that they name: doc_starts[0] is 1; a 1 at tile i means a document starts at token 64 * i.
All inputs are finite; a program needn't handle non-finite values.
Results may differ from a plain program's by a relative error of at most 0.0057.
Values may be sent and summed in bfloat16 or wider, within the bound.
No kernel may reach another device: no remote copies, remote signals or barrier semaphores. Data moves between devices by JAX's collectives and lax.ppermute only.
A program may use at most 128 MiB of HBM per device.

v0:
```python
import functools

import jax
import jax.numpy as jnp
from jax import lax
from jax.experimental import pallas as pl
from jax.experimental.pallas import tpu as pltpu
from jax.sharding import PartitionSpec as P


D = 8192
MODES = 8
TILE = 64
LANES = 128
ROWS = 8
PAIR = 2 * ROWS
PITCH = TILE + MODES

GROUP_ROWS = 24
GAIN, SKIP = 16, 17
F32 = jnp.float32
BF16 = jnp.bfloat16
HIGHEST = lax.Precision.HIGHEST
SEND = BF16
UNROLL = 16


def rounded(array):
    return array.astype(BF16).astype(F32)


def lane_group(group):
    return slice(group * LANES, (group + 1) * LANES)


def rows_of(tile):
    return slice(tile * MODES, (tile + 1) * MODES)


def survive(starts_ref, index):
    return (1 - starts_ref[index]).astype(F32)


def keeps(starts_ref, first, count):
    found = starts_ref[first]
    for step in range(1, count):
        found = found + starts_ref[first + step]
    return jnp.where(found == 0, 1.0, 0.0)


def total(parts):
    parts = list(parts)
    while len(parts) > 1:
        parts = [sum(parts[i : i + 2][1:], parts[i]) for i in range(0, len(parts), 2)]
    return parts[0]


def wide(table, m):
    return jnp.broadcast_to(table[m : m + 1], (ROWS, LANES))


def per_mode(table):
    return [wide(table, m) for m in range(MODES)]


def phase_powers(rate, first, sign):
    power = lax.broadcasted_iota(jnp.int32, (ROWS, LANES), 0).astype(F32) * sign + first
    return [jnp.exp(-wide(rate, m) * power) for m in range(MODES)]


def weighted(powers, table):
    return [p * wide(table, m) for m, p in enumerate(powers)]


def advance(factors, states, x):
    return tuple(f * s + x for f, s in zip(factors, states))


class Copies:
    def __init__(self, sems):
        self.sems, self.used = sems, 0

    def start(self, source, target):
        copy = pltpu.make_async_copy(source, target, self.sems.at[self.used])
        self.used += 1
        copy.start()
        return copy


def send_state(states, send_ref):
    block = jnp.concatenate(states, axis=0).astype(send_ref.dtype)
    for other in range(send_ref.shape[0]):
        send_ref[other] = block


def gather_phases(states, powers):
    return jnp.concatenate(
        [jnp.sum(s * p, axis=0, keepdims=True) for s, p in zip(states, powers)], axis=0
    )


def first_kernel(
    starts_hbm,
    key_hbm,
    value_hbm,
    rate_hbm,
    send_ref,
    starts_ref,
    key_ref,
    value_ref,
    rate_ref,
    sems,
):
    tokens, width = key_hbm.shape
    tiles, groups = tokens // TILE, width // LANES
    me = lax.axis_index("seq")
    copies = Copies(sems)
    large = []
    for group in range(groups):
        lanes = lane_group(group)
        large.append(
            [
                copies.start(key_hbm.at[:, lanes], key_ref.at[group]),
                copies.start(value_hbm.at[:, lanes], value_ref.at[group]),
            ]
        )
        if group == 0:
            small = [copies.start(rate_hbm, rate_ref), copies.start(starts_hbm, starts_ref)]
    for copy in small:
        copy.wait()
    fulls = []
    for first in range(0, groups, 2):
        pair = range(first, min(first + 2, groups))
        rates = [rate_ref[:, lane_group(group)] for group in pair]
        factors = [per_mode(jnp.exp(-rate * ROWS)) for rate in rates]
        for group in pair:
            for copy in large[group]:
                copy.wait()
        states = [(jnp.zeros((ROWS, LANES), F32),) * MODES for _ in pair]
        for tile in range(tiles):
            if tile:
                alive = survive(starts_ref, me * tiles + tile)
                states = [tuple(s * alive for s in state) for state in states]
            for step in range(0, TILE, PAIR):
                rows = slice(tile * TILE + step, tile * TILE + step + PAIR)
                for index, group in enumerate(pair):
                    x = rounded(key_ref[group, rows, :].astype(F32) * value_ref[group, rows, :].astype(F32))
                    states[index] = advance(factors[index], states[index], x[:ROWS])
                    states[index] = advance(factors[index], states[index], x[ROWS:])
        for rate, state in zip(rates, states):
            fulls.append(gather_phases(state, phase_powers(rate, ROWS - 1, -1)))
    send_state(fulls, send_ref)


def per_tile(table, tiles):
    return [jnp.broadcast_to(table[m : m + 1], (tiles, LANES)) for m in range(MODES)]


def over_tile(step, first, reverse):
    def body(index, carry):
        return step(TILE - 1 - index if reverse else index, carry)

    return lax.fori_loop(0, TILE, body, first, unroll=UNROLL)


def tile_rows(tile, count=TILE, first=0):
    return slice(tile * PITCH + first, tile * PITCH + first + count)


def put_tiles(ref, group, data):
    for tile in range(data.shape[0] // TILE):
        ref[group, tile_rows(tile), :] = data[tile * TILE : (tile + 1) * TILE]


def local_conv(me, starts_ref, rate, weight, skip, data_ref, work_ref, conv_ref, group, reverse):
    tiles = data_ref.shape[1] // PITCH
    factors, weights = per_tile(jnp.exp(-rate), tiles), per_tile(weight, tiles)
    skip = jnp.broadcast_to(skip, (tiles, LANES))

    def rows(offset):
        return pl.ds(offset, tiles, stride=PITCH)

    def leave(offset, states):
        return advance(factors, states, data_ref[group, rows(offset), :])

    ends = over_tile(leave, (jnp.zeros((tiles, LANES), F32),) * MODES, reverse)
    for m in range(MODES):
        work_ref[group, rows(TILE + m), :] = ends[m]
    tile_decay = jnp.exp(-rate * TILE)
    state = jnp.zeros((MODES, LANES), F32)
    for tile in reversed(range(tiles)) if reverse else range(tiles):
        alive = survive(starts_ref, me * tiles + tile)
        here = tile_rows(tile, MODES, TILE)
        end = work_ref[group, here, :]
        if reverse:
            work_ref[group, here, :] = state
            state = (end + tile_decay * state) * alive
        else:
            state = state * alive
            work_ref[group, here, :] = state
            state = end + tile_decay * state

    def step(offset, states):
        x = data_ref[group, rows(offset), :]
        states = advance(factors, states, x)
        work_ref[group, rows(offset), :] = total(w * s for w, s in zip(weights, states)) + skip * x
        return states

    over_tile(step, tuple(work_ref[group, rows(TILE + m), :] for m in range(MODES)), reverse)
    for tile in range(tiles):
        conv_ref[group, tile * TILE : (tile + 1) * TILE, :] = work_ref[group, tile_rows(tile), :]


def table_rows(tiles, groups, parts):
    return groups * GROUP_ROWS + tiles + parts


def put_flag(ref, row, value):
    ref[row : row + 1, :] = jnp.full((1, LANES), value)


def get_flag(ref, row):
    return jnp.broadcast_to(ref[row : row + 1, :], (ROWS, LANES))


class Table:
    def __init__(self, ref, tiles, groups):
        self.ref, self.groups = ref, groups
        self.flags = groups * GROUP_ROWS
        self.parts = self.flags + tiles

    def rows(self, group, first, count):
        first += group * GROUP_ROWS
        return slice(first, first + count)

    def rate(self, group):
        return self.ref[self.rows(group, 0, MODES), :]

    def weight(self, group):
        return self.ref[self.rows(group, MODES, MODES), :]

    def gain(self, group):
        return self.ref[self.rows(group, GAIN, 1), :]

    def skip(self, group):
        return self.ref[self.rows(group, SKIP, 1), :]

    def alive(self, tile):
        return get_flag(self.ref, self.flags + tile)

    def kept(self, part):
        return get_flag(self.ref, self.parts + part)


def forward_local_kernel(
    starts_ref,
    key_ref,
    value_ref,
    rate_ref,
    weight_ref,
    gain_ref,
    skip_ref,
    conv_ref,
    table_ref,
    data_ref,
    work_ref,
):
    tokens, width = key_ref.shape
    tiles, groups = tokens // TILE, width // LANES
    me = lax.axis_index("seq")
    table = Table(table_ref, tiles, groups)
    for group in range(groups):
        lanes = lane_group(group)
        put_tiles(data_ref, group, rounded(key_ref[:, lanes].astype(F32) * value_ref[:, lanes].astype(F32)))
        rate, weight, skip = rate_ref[:, lanes], weight_ref[:, lanes], skip_ref[:, lanes]
        local_conv(me, starts_ref, rate, weight, skip, data_ref, work_ref, conv_ref, group, False)
        table_ref[table.rows(group, 0, MODES), :] = rate
        table_ref[table.rows(group, MODES, MODES), :] = weight
        table_ref[table.rows(group, GAIN, 1), :] = gain_ref[:, lanes]
        table_ref[table.rows(group, SKIP, 1), :] = skip
    for tile in range(tiles):
        put_flag(table_ref, table.flags + tile, survive(starts_ref, me * tiles + tile))
    for part in range(starts_ref.shape[0] // tiles):
        put_flag(table_ref, table.parts + part, keeps(starts_ref, part * tiles, tiles))


def token_sums(array):
    return [
        lax.dot_general(
            jnp.ones((ROWS, LANES), F32),
            array[lane_group(block)],
            (((1,), (1,)), ((), ())),
            precision=HIGHEST,
            preferred_element_type=F32,
        )
        for block in range(array.shape[0] // LANES)
    ]


def part_of(got_ref, part, groups):
    return [got_ref[part, rows_of(group), :].astype(F32) for group in range(groups)]


def forward_join_kernel(
    table_ref,
    got_ref,
    conv_ref,
    query_ref,
    cot_ref,
    mixer_ref,
    sums_ref,
    square_ref,
    inner_ref,
):
    tokens, width = query_ref.shape
    tiles, groups = tokens // TILE, width // LANES
    table = Table(table_ref, tiles, groups)
    parts = got_ref.shape[0]
    me = lax.axis_index("seq")
    rates = [table.rate(group) for group in range(groups)]
    part_decay = [jnp.exp(-rate * tokens) for rate in rates]
    states = [jnp.zeros((MODES, LANES), F32)] * groups
    for part in range(parts - 1):
        kept = table.kept(part)
        arrived = part_of(got_ref, part, groups)
        states = [
            jnp.where(part < me, a + d * kept * s, s) for a, d, s in zip(arrived, part_decay, states)
        ]
    for group in range(groups):
        lanes = lane_group(group)
        factors = per_mode(jnp.exp(-rates[group] * ROWS))
        carry = weighted(phase_powers(rates[group], 1, 1), states[group] * table.weight(group))
        gain = jnp.broadcast_to(table.gain(group), (PAIR, LANES))
        for tile in range(tiles):
            alive = table.alive(tile)
            carry = [c * alive for c in carry]
            for step in range(0, TILE, PAIR):
                rows = slice(tile * TILE + step, tile * TILE + step + PAIR)
                extra = []
                for _ in range(2):
                    extra.append(total(carry))
                    carry = [c * f for c, f in zip(carry, factors)]
                mixer = (conv_ref[group, rows, :] + jnp.concatenate(extra, axis=0)).astype(BF16)
                mixer_ref[rows, lanes] = mixer
                gated = query_ref[rows, lanes].astype(F32) * mixer.astype(F32)
                square = gated * gated
                inner = cot_ref[rows, lanes].astype(F32) * gain * gated
                if group:
                    square, inner = square + square_ref[rows, :], inner + inner_ref[rows, :]
                square_ref[rows, :] = square
                inner_ref[rows, :] = inner
    sums = token_sums(square_ref[...]) + token_sums(inner_ref[...])
    row = lax.broadcasted_iota(jnp.int32, (ROWS, LANES), 0)
    block = sums[0]
    for index in range(1, len(sums)):
        block = jnp.where(row == index, sums[index], block)
    for other in range(sums_ref.shape[0]):
        sums_ref[other] = block


def spread_sums(sums, scale_ref, shift_ref):
    blocks = scale_ref.shape[0] // LANES
    rinv = lax.rsqrt(sums / D + 1e-05)
    lean = jnp.concatenate([sums[blocks:], sums[:blocks]], axis=0)
    lean = rinv * rinv * rinv * lean / D
    rinv, lean = jnp.transpose(rinv), jnp.transpose(lean)
    for block in range(blocks):
        rows = lane_group(block)
        scale_ref[rows, :] = jnp.broadcast_to(rinv[:, block : block + 1], (LANES, LANES))
        shift_ref[rows, :] = jnp.broadcast_to(lean[:, block : block + 1], (LANES, LANES))


def backward_kernel(
    table_ref,
    sums_ref,
    query_ref,
    cot_ref,
    mixer_ref,
    adjoint_ref,
    send_ref,
    totals_ref,
    scale_ref,
    shift_ref,
):
    tokens, width = query_ref.shape
    tiles, groups = tokens // TILE, width // LANES
    table = Table(table_ref, tiles, groups)
    sums = total(sums_ref[other] for other in range(sums_ref.shape[0]))
    totals_ref[...] = sums
    spread_sums(sums, scale_ref, shift_ref)
    fulls = []
    for group in range(groups):
        lanes = lane_group(group)
        rate = table.rate(group)
        factors = per_mode(jnp.exp(-rate * ROWS))
        powers = phase_powers(rate, 0, 1)
        gain = jnp.broadcast_to(table.gain(group), (PAIR, LANES))
        states = (jnp.zeros((ROWS, LANES), F32),) * MODES
        for tile in reversed(range(tiles)):
            if tile < tiles - 1:
                alive = table.alive(tile + 1)
                states = tuple(s * alive for s in states)
            for step in reversed(range(0, TILE, PAIR)):
                rows = slice(tile * TILE + step, tile * TILE + step + PAIR)
                query = query_ref[rows, lanes].astype(F32)
                gated = query * mixer_ref[rows, lanes].astype(F32)
                scaled = cot_ref[rows, lanes].astype(F32) * gain
                adjoint = ((scale_ref[rows, :] * scaled - gated * shift_ref[rows, :]) * query).astype(BF16)
                adjoint_ref[rows, lanes] = adjoint
                x = adjoint.astype(F32)
                states = advance(factors, states, x[ROWS:])
                states = advance(factors, states, x[:ROWS])
        fulls.append(gather_phases(states, powers))
    send_state(fulls, send_ref)


def outputs_kernel(
    table_ref, totals_ref, query_ref, cot_ref, mixer_ref, mixed_ref, grad_query_ref, done_ref, scale_ref, shift_ref
):
    tokens, width = query_ref.shape
    tiles, groups = tokens // TILE, width // LANES
    table = Table(table_ref, tiles, groups)
    spread_sums(totals_ref[...], scale_ref, shift_ref)
    for group in range(groups):
        lanes = lane_group(group)
        gain = jnp.broadcast_to(table.gain(group), (TILE, LANES))
        for tile in range(tiles):
            rows = slice(tile * TILE, (tile + 1) * TILE)
            scale, shift = scale_ref[rows, :], shift_ref[rows, :]
            mixer = mixer_ref[rows, lanes].astype(F32)
            gated = query_ref[rows, lanes].astype(F32) * mixer
            scaled = cot_ref[rows, lanes].astype(F32) * gain
            mixed_ref[rows, lanes] = (gated * scale * gain).astype(BF16)
            grad_query_ref[rows, lanes] = ((scale * scaled - gated * shift) * mixer).astype(BF16)
    done_ref[...] = totals_ref[...]


def backward_local_kernel(
    starts_ref, table_ref, adjoint_ref, done_ref, conv_ref, flags_ref, data_ref, work_ref
):
    tokens, width = adjoint_ref.shape
    tiles, groups = tokens // TILE, width // LANES
    me = lax.axis_index("seq")
    table = Table(table_ref, tiles, groups)
    for group in range(groups):
        put_tiles(data_ref, group, adjoint_ref[:, lane_group(group)].astype(F32))
        rate, weight, skip = table.rate(group), table.weight(group), table.skip(group)
        local_conv(me, starts_ref, rate, weight, skip, data_ref, work_ref, conv_ref, group, True)
    for part in range(starts_ref.shape[0] // tiles):
        put_flag(flags_ref, 2 * part, keeps(starts_ref, part * tiles + 1, tiles - 1))
        put_flag(flags_ref, 2 * part + 1, survive(starts_ref, part * tiles))


def backward_join_kernel(
    table_ref,
    flags_ref,
    got_ref,
    conv_ref,
    key_ref,
    value_ref,
    grad_key_hbm,
    grad_value_hbm,
    grad_key_ref,
    grad_value_ref,
    sems,
):
    tokens, width = key_ref.shape
    tiles, groups = tokens // TILE, width // LANES
    table = Table(table_ref, tiles, groups)
    parts = got_ref.shape[0]
    me = lax.axis_index("seq")
    copies = Copies(sems)
    rates = [table.rate(group) for group in range(groups)]
    part_decay = [jnp.exp(-rate * tokens) for rate in rates]
    states = [jnp.zeros((MODES, LANES), F32)] * groups
    for part in range(parts - 1, 0, -1):
        inner, alive = get_flag(flags_ref, 2 * part), get_flag(flags_ref, 2 * part + 1)
        arrived = part_of(got_ref, part, groups)
        states = [
            jnp.where(part > me, (a + d * inner * s) * alive, s)
            for a, d, s in zip(arrived, part_decay, states)
        ]
    out = []
    for group in range(groups):
        lanes = lane_group(group)
        factors = per_mode(jnp.exp(-rates[group] * ROWS))
        carry = weighted(phase_powers(rates[group], ROWS, -1), states[group] * table.weight(group))
        for tile in reversed(range(tiles)):
            if tile < tiles - 1:
                alive = table.alive(tile + 1)
                carry = [c * alive for c in carry]
            for step in reversed(range(0, TILE, PAIR)):
                rows = slice(tile * TILE + step, tile * TILE + step + PAIR)
                extra = []
                for _ in range(2):
                    extra.append(total(carry))
                    carry = [c * f for c, f in zip(carry, factors)]
                dproduct = rounded(conv_ref[group, rows, :] + jnp.concatenate(extra[::-1], axis=0))
                grad_key_ref[group, rows, :] = (dproduct * value_ref[rows, lanes].astype(F32)).astype(BF16)
                grad_value_ref[group, rows, :] = (dproduct * key_ref[rows, lanes].astype(F32)).astype(BF16)
        out.append(copies.start(grad_key_ref.at[group], grad_key_hbm.at[:, lanes]))
        out.append(copies.start(grad_value_ref.at[group], grad_value_hbm.at[:, lanes]))
    for copy in out:
        copy.wait()


def scratch_of(item):
    if isinstance(item, tuple):
        return pltpu.VMEM(*item) if isinstance(item[0], tuple) else pltpu.VMEM(item, F32)
    return item


def call(kernel, ins, outs, scratch, work, vmem=16):
    return pl.pallas_call(
        kernel,
        out_shape=[jax.ShapeDtypeStruct(*out[:2]) for out in outs],
        in_specs=[pl.BlockSpec(memory_space=space) for _, space in ins],
        out_specs=[pl.BlockSpec(memory_space=(*out, pltpu.VMEM)[2]) for out in outs],
        scratch_shapes=[scratch_of(item) for item in scratch],
        compiler_params=pltpu.CompilerParams(vmem_limit_bytes=vmem * 1024 * 1024),
        cost_estimate=pl.CostEstimate(flops=work, bytes_accessed=work // 8, transcendentals=0),
    )(*[array for array, _ in ins])


def on_device(
    query_feat,
    key_feat,
    value_feat,
    decay_rate,
    residues,
    skip_gain,
    norm_gain,
    doc_starts,
    cotangent,
):
    tokens, width = query_feat.shape
    parts, peers = lax.axis_size("seq"), lax.axis_size("chan")
    tiles, groups = tokens // TILE, width // LANES
    starts = (doc_starts, pltpu.SMEM)
    weight = residues * jnp.sqrt(-jnp.expm1(-2.0 * decay_rate))
    skip, gain = skip_gain[None], norm_gain[None]
    whole, split, pitched = (tokens, width), (groups, tokens, LANES), (groups, tiles * PITCH, LANES)
    block, spread, summed = (parts, groups * MODES, LANES), (tokens, LANES), (peers, ROWS, LANES)
    modes, packed = (MODES, width), (table_rows(tiles, groups, parts), LANES)
    work = tokens * width

    def vmem(*arrays):
        return [(array, pltpu.VMEM) for array in arrays]

    def hbm(*arrays):
        return [(array, pl.ANY) for array in arrays]

    def sems(count):
        return pltpu.SemaphoreType.DMA((count,))

    (send,) = call(
        first_kernel,
        hbm(doc_starts, key_feat, value_feat, decay_rate),
        [(block, SEND)],
        [
            pltpu.SMEM(doc_starts.shape, jnp.int32),
            (split, BF16),
            (split, BF16),
            modes,
            sems(2 * groups + 2),
        ],
        work * 20,
        60,
    )
    got = lax.all_to_all(send, "seq", 0, 0)
    conv, table = call(
        forward_local_kernel,
        [starts] + vmem(key_feat, value_feat, decay_rate, weight, gain, skip),
        [(split, F32), (packed, F32)],
        [pitched, pitched],
        work * 50,
    )
    mixer, sums = call(
        forward_join_kernel,
        vmem(table, got, conv, query_feat, cotangent),
        [(whole, BF16), (summed, F32)],
        [spread, spread],
        work * 30,
    )
    sums = lax.all_to_all(sums, "chan", 0, 0)
    adjoint, send, totals = call(
        backward_kernel,
        vmem(table, sums, query_feat, cotangent, mixer),
        [(whole, BF16), (block, SEND), ((ROWS, LANES), F32)],
        [spread, spread],
        work * 30,
    )
    got = lax.all_to_all(send, "seq", 0, 0)
    mixed, grad_query, done = call(
        outputs_kernel,
        vmem(table, totals, query_feat, cotangent, mixer),
        [(whole, BF16), (whole, BF16), ((ROWS, LANES), F32)],
        [spread, spread],
        work * 20,
    )
    conv, flags = call(
        backward_local_kernel,
        [starts] + vmem(table, adjoint, done),
        [(split, F32), ((2 * parts, LANES), F32)],
        [pitched, pitched],
        work * 50,
    )
    grad_key, grad_value = call(
        backward_join_kernel,
        vmem(table, flags, got, conv, key_feat, value_feat),
        [(whole, BF16, pl.ANY), (whole, BF16, pl.ANY)],
        [(split, BF16), (split, BF16), sems(2 * groups)],
        work * 30,
    )
    return mixed, grad_query, grad_key, grad_value


def solution(mesh):
    both = P("seq", "chan")
    in_specs = (
        both,
        both,
        both,
        P(None, "chan"),
        P(None, "chan"),
        P("chan"),
        P("chan"),
        P(),
        both,
    )
    return jax.shard_map(
        on_device, mesh=mesh, in_specs=in_specs, out_specs=(both,) * 4, check_vma=False
    )
```

profile of v0, /device:TPU:64, one launch (start us, length us, event | category | flops | bytes accessed | tf_op | source)
XLA Modules:
  0.0 67.6 jit_solution(6004617920836670100)
XLA Ops:
  0.6 0.0 copy-start.7
  0.6 0.0 copy-start.11
  0.7 0.0 copy-start.3
  0.7 2.8 %shard_map.121 = bf16[32,32,128]{2,1,0:T(8,128)(2,1)} custom-call(s32[256]{0:T(256)} %starts_ref.3, bf16[512,512]{1,0:T(8,128)(2,1)} %key_ref.3, bf16[512,512]{1,0:T(8,128)(2,1)} %value_ref.3, f32[8,512]{1,0:T(8,128)} %rate_hbm.1), custom_call_target="tpu_custom_call" | custom-call | flops 5242880 | bytes 655360 | tf_op jit(solution)/shard_map/pallas_call | solution.py:514
  3.4 0.0 copy-start.2
  3.5 12.7 %all-to-all-start = ((bf16[32,32,128]{2,1,0:T(8,128)(2,1)}), bf16[32,32,128]{2,1,0:T(8,128)(2,1)S(1)}, u32[]{:S(2)}, u32[]{:S(2)}) async-start(bf16[32,32,128]{2,1,0:T(8,128)(2,1)} %shard_map.121), calls=%async_computation | async-start | bytes 524288 | tf_op jit(solution)/shard_map/all_to_all | solution.py:570
  16.2 0.0 copy-done.7
  16.2 0.0 copy-done.11
  16.2 0.0 copy-start.10
  16.3 0.0 copy-start.9
  16.3 0.0 copy-start.8
  16.3 0.0 copy-done.3
  16.3 0.0 copy-done.2
  16.3 0.6 copy-done.10
  16.9 0.0 copy-done.9
  16.9 0.0 copy-done.8
  17.0 0.0 copy-start
  17.0 0.0 copy-start.1
  17.0 3.0 %shard_map.120 = (f32[4,512,128]{2,1,0:T(8,128)S(1)}, f32[136,128]{1,0:T(8,128)S(1)}) custom-call(s32[256]{0:T(256)S(1)} %copy-done.8, bf16[512,512]{1,0:T(8,128)(2,1)S(1)} %copy-done.2, bf16[512,512]{1,0:T(8,128)(2,1)S(1)} %copy-done.3, f32[8,512]{1,0:T(8,128)S(1)} %copy-done.7, f32[8,512]{1,0:T(8,128)S(1)} %sqrt_multiply_fusion.weight_ref, ...), custom_call_target="tpu_custom_call" | custom-call | flops 13107200 | bytes 1638400 | tf_op jit(solution)/shard_map/pallas_call | solution.py:514
  20.0 0.0 copy-start.4
  20.0 1.0 %copy-done.4 = f32[4,512,128]{2,1,0:T(8,128)} copy-done((f32[4,512,128]{2,1,0:T(8,128)}, f32[4,512,128]{2,1,0:T(8,128)S(1)}, u32[]{:S(2)}) %copy-start.4) | copy-done | bytes 1048600
  21.0 7.5 %all-to-all-done.got_ref = bf16[32,32,128]{2,1,0:T(8,128)(2,1)S(1)} async-done(((bf16[32,32,128]{2,1,0:T(8,128)(2,1)}), bf16[32,32,128]{2,1,0:T(8,128)(2,1)S(1)}, u32[]{:S(2)}, u32[]{:S(2)}) %all-to-all-start) | async-done | bytes 262176 | tf_op jit(solution)/shard_map/all_to_all | solution.py:570
  28.5 0.0 copy-done
  28.5 0.0 copy-done.1
  28.5 0.0 copy-start.5
  28.5 1.2 %copy-done.5 = f32[4,512,128]{2,1,0:T(8,128)S(1)} copy-done((f32[4,512,128]{2,1,0:T(8,128)S(1)}, f32[4,512,128]{2,1,0:T(8,128)}, u32[]{:S(2)}) %copy-start.5) | copy-done | bytes 1048600
  29.7 1.8 %shard_map.122 = (bf16[512,512]{1,0:T(8,128)(2,1)S(1)}, f32[16,8,128]{2,1,0:T(8,128)S(1)}) custom-call(f32[136,128]{1,0:T(8,128)S(1)} %get-tuple-element.18.table_ref, bf16[32,32,128]{2,1,0:T(8,128)(2,1)S(1)} %all-to-all-done.got_ref, f32[4,512,128]{2,1,0:T(8,128)S(1)} %copy-done.5, bf16[512,512]{1,0:T(8,128)(2,1)S(1)} %copy-done, bf16[512,512]{1,0:T(8,128)(2,1)S(1)} %copy-done.1), custom_call_target="tpu_custom_call" | custom-call | flops 7864320 | bytes 983040 | tf_op jit(solution)/shard_map/pallas_call | solution.py:514
  31.5 14.9 %all_to_all.15.sums_ref = f32[16,8,128]{2,1,0:T(8,128)S(1)} all-to-all(f32[16,8,128]{2,1,0:T(8,128)S(1)} %get-tuple-element.20), channel_id=1, replica_groups=mesh['seq'=32,'chan'=16] {'chan'}, dimensions={0} | all-to-all | bytes 131072 | tf_op jit(solution)/shard_map/all_to_all | solution.py:585
  46.4 1.3 %shard_map.123 = (bf16[512,512]{1,0:T(8,128)(2,1)S(1)}, bf16[32,32,128]{2,1,0:T(8,128)(2,1)S(1)}, f32[8,128]{1,0:T(8,128)S(1)}) custom-call(f32[136,128]{1,0:T(8,128)S(1)} %get-tuple-element.18.table_ref, f32[16,8,128]{2,1,0:T(8,128)S(1)} %all_to_all.15.sums_ref, bf16[512,512]{1,0:T(8,128)(2,1)S(1)} %copy-done, bf16[512,512]{1,0:T(8,128)(2,1)S(1)} %copy-done.1, ...), custom_call_target="tpu_custom_call" | custom-call | flops 7864320 | bytes 983040 | tf_op jit(solution)/shard_map/pallas_call | solution.py:514
  47.6 0.0 copy-start.6
  47.6 0.7 %copy-done.6 = bf16[32,32,128]{2,1,0:T(8,128)(2,1)} copy-done((bf16[32,32,128]{2,1,0:T(8,128)(2,1)}, bf16[32,32,128]{2,1,0:T(8,128)(2,1)S(1)}, u32[]{:S(2)}) %copy-start.6) | copy-done | bytes 262168
  48.3 4.6 %all-to-all-start.2 = ((bf16[32,32,128]{2,1,0:T(8,128)(2,1)}), bf16[32,32,128]{2,1,0:T(8,128)(2,1)S(1)}, u32[]{:S(2)}, u32[]{:S(2)}) async-start(bf16[32,32,128]{2,1,0:T(8,128)(2,1)} %copy-done.6), calls=%async_computation.2 | async-start | bytes 524288 | tf_op jit(solution)/shard_map/all_to_all | solution.py:593
  52.9 1.6 %shard_map.124 = (bf16[512,512]{1,0:T(8,128)(2,1)}, bf16[512,512]{1,0:T(8,128)(2,1)}, f32[8,128]{1,0:T(8,128)S(1)}) custom-call(f32[136,128]{1,0:T(8,128)S(1)} %get-tuple-element.18.table_ref, f32[8,128]{1,0:T(8,128)S(1)} %get-tuple-element.22.totals_ref, bf16[512,512]{1,0:T(8,128)(2,1)S(1)} %copy-done, bf16[512,512]{1,0:T(8,128)(2,1)S(1)} %copy-done.1, ...), custom_call_target="tpu_custom_call" | custom-call | flops 5242880 | bytes 655360 | tf_op jit(solution)/shard_map/pallas_call | solution.py:514
  54.5 3.0 %shard_map.125 = (f32[4,512,128]{2,1,0:T(8,128)S(1)}, f32[64,128]{1,0:T(8,128)S(1)}) custom-call(s32[256]{0:T(256)S(1)} %copy-done.8, f32[136,128]{1,0:T(8,128)S(1)} %get-tuple-element.18.table_ref, bf16[512,512]{1,0:T(8,128)(2,1)S(1)} %get-tuple-element.25.adjoint_ref, f32[8,128]{1,0:T(8,128)S(1)} %get-tuple-element.26.done_ref), custom_call_target="tpu_custom_call" | custom-call | flops 13107200 | bytes 1638400 | tf_op jit(solution)/shard_map/pallas_call | solution.py:514
  57.5 8.2 %all-to-all-done.2.got_ref = bf16[32,32,128]{2,1,0:T(8,128)(2,1)S(1)} async-done(((bf16[32,32,128]{2,1,0:T(8,128)(2,1)}), bf16[32,32,128]{2,1,0:T(8,128)(2,1)S(1)}, u32[]{:S(2)}, u32[]{:S(2)}) %all-to-all-start.2) | async-done | bytes 262176 | tf_op jit(solution)/shard_map/all_to_all | solution.py:593
  65.7 1.9 %shard_map.126 = (bf16[512,512]{1,0:T(8,128)(2,1)}, bf16[512,512]{1,0:T(8,128)(2,1)}) custom-call(f32[136,128]{1,0:T(8,128)S(1)} %get-tuple-element.18.table_ref, f32[64,128]{1,0:T(8,128)S(1)} %get-tuple-element.27.flags_ref, bf16[32,32,128]{2,1,0:T(8,128)(2,1)S(1)} %all-to-all-done.2.got_ref, f32[4,512,128]{2,1,0:T(8,128)S(1)} %get-tuple-element.29.conv_ref, ...), custom_call_target="tpu_custom_call" | custom-call | flops 7864320 | bytes 983040 | tf_op jit(solution)/shard_map/pallas_call | solution.py:514
  (1 shorter events, 0.0 us)
Async XLA Ops:
  0.6 15.6 %copy-start.7 = (f32[8,512]{1,0:T(8,128)S(1)}, f32[8,512]{1,0:T(8,128)}, u32[]{:S(2)}) copy-start(f32[8,512]{1,0:T(8,128)} %rate_hbm.1) | copy-start | bytes 49156
  0.6 15.6 %copy-start.11 = (f32[8,512]{1,0:T(8,128)S(1)}, f32[8,512]{1,0:T(8,128)}, u32[]{:S(2)}) copy-start(f32[8,512]{1,0:T(8,128)} %param.13) | copy-start | bytes 49156
  0.7 15.6 %copy-start.3 = (bf16[512,512]{1,0:T(8,128)(2,1)S(1)}, bf16[512,512]{1,0:T(8,128)(2,1)}, u32[]{:S(2)}) copy-start(bf16[512,512]{1,0:T(8,128)(2,1)} %value_ref.3) | copy-start | bytes 1572868
  3.4 12.8 %copy-start.2 = (bf16[512,512]{1,0:T(8,128)(2,1)S(1)}, bf16[512,512]{1,0:T(8,128)(2,1)}, u32[]{:S(2)}) copy-start(bf16[512,512]{1,0:T(8,128)(2,1)} %key_ref.3) | copy-start | bytes 1572868
  3.5 25.0 %all-to-all-start = ((bf16[32,32,128]{2,1,0:T(8,128)(2,1)}), bf16[32,32,128]{2,1,0:T(8,128)(2,1)S(1)}, u32[]{:S(2)}, u32[]{:S(2)}) async-start(bf16[32,32,128]{2,1,0:T(8,128)(2,1)} %shard_map.121), calls=%async_computation | async-start | bytes 524288 | tf_op jit(solution)/shard_map/all_to_all | solution.py:570
  16.2 0.7 %copy-start.10 = (f32[512]{0:T(512)S(1)}, f32[512]{0:T(512)}, u32[]{:S(2)}) copy-start(f32[512]{0:T(512)} %param.14) | copy-start | bytes 6148
  16.3 0.7 %copy-start.9 = (f32[512]{0:T(512)S(1)}, f32[512]{0:T(512)}, u32[]{:S(2)}) copy-start(f32[512]{0:T(512)} %param.15) | copy-start | bytes 6148
  16.3 0.7 %copy-start.8 = (s32[256]{0:T(256)S(1)}, s32[256]{0:T(256)}, u32[]{:S(2)}) copy-start(s32[256]{0:T(256)} %starts_ref.3) | copy-start | bytes 3076
  17.0 11.5 %copy-start = (bf16[512,512]{1,0:T(8,128)(2,1)S(1)}, bf16[512,512]{1,0:T(8,128)(2,1)}, u32[]{:S(2)}) copy-start(bf16[512,512]{1,0:T(8,128)(2,1)} %query_ref.5) | copy-start | bytes 1572868
  17.0 11.5 %copy-start.1 = (bf16[512,512]{1,0:T(8,128)(2,1)S(1)}, bf16[512,512]{1,0:T(8,128)(2,1)}, u32[]{:S(2)}) copy-start(bf16[512,512]{1,0:T(8,128)(2,1)} %cot_ref.5) | copy-start | bytes 1572868
  20.0 1.0 %copy-start.4 = (f32[4,512,128]{2,1,0:T(8,128)}, f32[4,512,128]{2,1,0:T(8,128)S(1)}, u32[]{:S(2)}) copy-start(f32[4,512,128]{2,1,0:T(8,128)S(1)} %get-tuple-element.19.conv_ref) | copy-start | bytes 3145732
  28.5 1.2 %copy-start.5 = (f32[4,512,128]{2,1,0:T(8,128)S(1)}, f32[4,512,128]{2,1,0:T(8,128)}, u32[]{:S(2)}) copy-start(f32[4,512,128]{2,1,0:T(8,128)} %copy-done.4) | copy-start | bytes 3145732
  47.6 0.7 %copy-start.6 = (bf16[32,32,128]{2,1,0:T(8,128)(2,1)}, bf16[32,32,128]{2,1,0:T(8,128)(2,1)S(1)}, u32[]{:S(2)}) copy-start(bf16[32,32,128]{2,1,0:T(8,128)(2,1)S(1)} %get-tuple-element.28) | copy-start | bytes 786436
  48.3 17.4 %all-to-all-start.2 = ((bf16[32,32,128]{2,1,0:T(8,128)(2,1)}), bf16[32,32,128]{2,1,0:T(8,128)(2,1)S(1)}, u32[]{:S(2)}, u32[]{:S(2)}) async-start(bf16[32,32,128]{2,1,0:T(8,128)(2,1)} %copy-done.6), calls=%async_computation.2 | async-start | bytes 524288 | tf_op jit(solution)/shard_map/all_to_all | solution.py:593
where the time goes:
time: 68 us; the launch traced here: 67.6 us
  starting transfers between devices  17.3 us (25%)
  waiting for transfers between devices  15.7 us (23%)
  Pallas kernels  15.3 us (22%)
  blocking collectives  14.9 us (22%)
  local copies, waits for them, and re-layouts  3.59 us (5%)
  between operations  0.8 us (1%)
    all_to_all x2, starting transfers between devices, on_device(): got = lax.all_to_all(send, 'seq', 0, 0)  17.3 us
    all_to_all x2, waiting for transfers between devices, on_device(): got = lax.all_to_all(send, 'seq', 0, 0)  15.7 us
    pallas_call x7, Pallas kernels, call(): pl.pallas_call(kernel, out_shape=[jax.ShapeDtypeStruct(*out[:2]) for out...  15.3 us
    all_to_all x1, blocking collectives, on_device(): sums = lax.all_to_all(sums, 'chan', 0, 0)  14.9 us
    unnamed x24, local copies, waits for them, and re-layouts  3.59 us
  transfers between devices with their start and end apart: 2, of which 2 were waited for; matrix products, arithmetic and copies ran while one was open for 0% of the time, Pallas kernels for 11%

commit v1 on v0

--- a/solution.py
+++ b/solution.py
@@ -23,6 +23,7 @@
 HIGHEST = lax.Precision.HIGHEST
 SEND = BF16
 UNROLL = 16
+LAG = 1
 
 
 def rounded(array):
@@ -129,26 +130,23 @@
     for copy in small:
         copy.wait()
     fulls = []
-    for first in range(0, groups, 2):
-        pair = range(first, min(first + 2, groups))
-        rates = [rate_ref[:, lane_group(group)] for group in pair]
-        factors = [per_mode(jnp.exp(-rate * ROWS)) for rate in rates]
-        for group in pair:
-            for copy in large[group]:
-                copy.wait()
-        states = [(jnp.zeros((ROWS, LANES), F32),) * MODES for _ in pair]
+    for group in range(groups):
+        rate = rate_ref[:, lane_group(group)]
+        factors = per_mode(jnp.exp(-rate * ROWS))
+        powers = phase_powers(rate, ROWS - 1, -1)
+        for copy in large[group]:
+            copy.wait()
+        states = (jnp.zeros((ROWS, LANES), F32),) * MODES
         for tile in range(tiles):
             if tile:
                 alive = survive(starts_ref, me * tiles + tile)
-                states = [tuple(s * alive for s in state) for state in states]
+                states = tuple(s * alive for s in states)
             for step in range(0, TILE, PAIR):
                 rows = slice(tile * TILE + step, tile * TILE + step + PAIR)
-                for index, group in enumerate(pair):
-                    x = rounded(key_ref[group, rows, :].astype(F32) * value_ref[group, rows, :].astype(F32))
-                    states[index] = advance(factors[index], states[index], x[:ROWS])
-                    states[index] = advance(factors[index], states[index], x[ROWS:])
-        for rate, state in zip(rates, states):
-            fulls.append(gather_phases(state, phase_powers(rate, ROWS - 1, -1)))
+                x = rounded(key_ref[group, rows, :].astype(F32) * value_ref[group, rows, :].astype(F32))
+                states = advance(factors, states, x[:ROWS])
+                states = advance(factors, states, x[ROWS:])
+        fulls.append(gather_phases(states, powers))
     send_state(fulls, send_ref)
 
 
@@ -455,21 +453,35 @@
     table_ref,
     flags_ref,
     got_ref,
+    conv_hbm,
+    key_hbm,
+    value_hbm,
+    grad_key_hbm,
+    grad_value_hbm,
     conv_ref,
     key_ref,
     value_ref,
-    grad_key_hbm,
-    grad_value_hbm,
+    dproduct_ref,
     grad_key_ref,
     grad_value_ref,
     sems,
 ):
-    tokens, width = key_ref.shape
+    tokens, width = key_hbm.shape
     tiles, groups = tokens // TILE, width // LANES
     table = Table(table_ref, tiles, groups)
     parts = got_ref.shape[0]
     me = lax.axis_index("seq")
     copies = Copies(sems)
+    near = [copies.start(conv_hbm.at[group], conv_ref.at[group]) for group in range(groups)]
+    large = []
+    for group in range(groups):
+        lanes = lane_group(group)
+        large.append(
+            [
+                copies.start(value_hbm.at[:, lanes], value_ref.at[group]),
+                copies.start(key_hbm.at[:, lanes], key_ref.at[group]),
+            ]
+        )
     rates = [table.rate(group) for group in range(groups)]
     part_decay = [jnp.exp(-rate * tokens) for rate in rates]
     states = [jnp.zeros((MODES, LANES), F32)] * groups
@@ -481,10 +493,22 @@
             for a, d, s in zip(arrived, part_decay, states)
         ]
     out = []
+
+    def finish(group):
+        lanes = lane_group(group)
+        for copy in large[group]:
+            copy.wait()
+        dproduct = dproduct_ref[group].astype(F32)
+        grad_key_ref[group] = (dproduct * value_ref[group].astype(F32)).astype(BF16)
+        out.append(copies.start(grad_key_ref.at[group], grad_key_hbm.at[:, lanes]))
+        grad_value_ref[group] = (dproduct * key_ref[group].astype(F32)).astype(BF16)
+        out.append(copies.start(grad_value_ref.at[group], grad_value_hbm.at[:, lanes]))
+
     for group in range(groups):
         lanes = lane_group(group)
         factors = per_mode(jnp.exp(-rates[group] * ROWS))
         carry = weighted(phase_powers(rates[group], ROWS, -1), states[group] * table.weight(group))
+        near[group].wait()
         for tile in reversed(range(tiles)):
             if tile < tiles - 1:
                 alive = table.alive(tile + 1)
@@ -495,11 +519,12 @@
                 for _ in range(2):
                     extra.append(total(carry))
                     carry = [c * f for c, f in zip(carry, factors)]
-                dproduct = rounded(conv_ref[group, rows, :] + jnp.concatenate(extra[::-1], axis=0))
-                grad_key_ref[group, rows, :] = (dproduct * value_ref[rows, lanes].astype(F32)).astype(BF16)
-                grad_value_ref[group, rows, :] = (dproduct * key_ref[rows, lanes].astype(F32)).astype(BF16)
-        out.append(copies.start(grad_key_ref.at[group], grad_key_hbm.at[:, lanes]))
-        out.append(copies.start(grad_value_ref.at[group], grad_value_hbm.at[:, lanes]))
+                dproduct = conv_ref[group, rows, :] + jnp.concatenate(extra[::-1], axis=0)
+                dproduct_ref[group, rows, :] = dproduct.astype(BF16)
+        if group >= LAG:
+            finish(group - LAG)
+    for group in range(groups - LAG, groups):
+        finish(group)
     for copy in out:
         copy.wait()
 
@@ -607,10 +632,11 @@
     )
     grad_key, grad_value = call(
         backward_join_kernel,
-        vmem(table, flags, got, conv, key_feat, value_feat),
+        vmem(table, flags, got) + hbm(conv, key_feat, value_feat),
         [(whole, BF16, pl.ANY), (whole, BF16, pl.ANY)],
-        [(split, BF16), (split, BF16), sems(2 * groups)],
+        [split] + [(split, BF16)] * 5 + [sems(5 * groups)],
         work * 30,
+        53,
     )
     return mixed, grad_query, grad_key, grad_value
 

time: 68 us -> 67.5 us (level)
  local copies, waits for them, and re-layouts: 3.59 us -> 1.66 us
  Pallas kernels: 15.3 us -> 16.7 us
    unnamed x24 -> x20, local copies, waits for them, and re-layouts: 3.59 us -> 1.66 us
    pallas_call x7, Pallas kernels: 15.3 us -> 16.7 us  [call(): pl.pallas_call(kernel, out_shape=[jax.ShapeDtypeStruct(*out[:2]) for out...]
where the time goes in v1:
time: 67.5 us; the launch traced here: 67.1 us
  starting transfers between devices  17.3 us (26%)
  Pallas kernels  16.7 us (25%)
  waiting for transfers between devices  15.7 us (23%)
  blocking collectives  14.9 us (22%)
  local copies, waits for them, and re-layouts  1.66 us (2%)
  between operations  0.78 us (1%)
    all_to_all x2, starting transfers between devices, on_device(): got = lax.all_to_all(send, 'seq', 0, 0)  17.3 us
    pallas_call x7, Pallas kernels, call(): pl.pallas_call(kernel, out_shape=[jax.ShapeDtypeStruct(*out[:2]) for out...  16.7 us
    all_to_all x2, waiting for transfers between devices, on_device(): got = lax.all_to_all(send, 'seq', 0, 0)  15.7 us
    all_to_all x1, blocking collectives, on_device(): sums = lax.all_to_all(sums, 'chan', 0, 0)  14.9 us
    unnamed x20, local copies, waits for them, and re-layouts  1.66 us
  transfers between devices with their start and end apart: 2, of which 2 were waited for; matrix products, arithmetic and copies ran while one was open for 0% of the time, Pallas kernels for 11%

profile of v1, /device:TPU:64, one launch (start us, length us, event | category | flops | bytes accessed | tf_op | source)
XLA Modules:
  0.0 67.1 jit_solution(14505211359810585465)
XLA Ops:
  0.6 0.0 copy-start.5
  0.6 0.0 copy-start.9
  0.7 0.0 copy-start.3
  0.7 2.6 %shard_map.121 = bf16[32,32,128]{2,1,0:T(8,128)(2,1)} custom-call(s32[256]{0:T(256)} %starts_ref.3, bf16[512,512]{1,0:T(8,128)(2,1)} %key_hbm.3, bf16[512,512]{1,0:T(8,128)(2,1)} %value_hbm.3, f32[8,512]{1,0:T(8,128)} %rate_hbm.1), custom_call_target="tpu_custom_call" | custom-call | flops 5242880 | bytes 655360 | tf_op jit(solution)/shard_map/pallas_call | solution.py:539
  3.3 0.0 copy-start.2
  3.3 12.7 %all-to-all-start = ((bf16[32,32,128]{2,1,0:T(8,128)(2,1)}), bf16[32,32,128]{2,1,0:T(8,128)(2,1)S(1)}, u32[]{:S(2)}, u32[]{:S(2)}) async-start(bf16[32,32,128]{2,1,0:T(8,128)(2,1)} %shard_map.121), calls=%async_computation | async-start | bytes 524288 | tf_op jit(solution)/shard_map/all_to_all | solution.py:595
  16.1 0.0 copy-done.5
  16.1 0.0 copy-done.9
  16.1 0.0 copy-start.8
  16.1 0.0 copy-start.7
  16.1 0.0 copy-start.6
  16.1 0.0 copy-done.3
  16.2 0.0 copy-done.2
  16.2 0.6 copy-done.8
  16.8 0.0 copy-done.7
  16.8 0.0 copy-done.6
  16.8 0.0 copy-start
  16.8 0.0 copy-start.1
  16.8 3.0 %shard_map.120 = (f32[4,512,128]{2,1,0:T(8,128)S(1)}, f32[136,128]{1,0:T(8,128)S(1)}) custom-call(s32[256]{0:T(256)S(1)} %copy-done.6, bf16[512,512]{1,0:T(8,128)(2,1)S(1)} %copy-done.2, bf16[512,512]{1,0:T(8,128)(2,1)S(1)} %copy-done.3, f32[8,512]{1,0:T(8,128)S(1)} %copy-done.5, f32[8,512]{1,0:T(8,128)S(1)} %sqrt_multiply_fusion.weight_ref, ...), custom_call_target="tpu_custom_call" | custom-call | flops 13107200 | bytes 1638400 | tf_op jit(solution)/shard_map/pallas_call | solution.py:539
  19.8 8.5 %all-to-all-done.got_ref = bf16[32,32,128]{2,1,0:T(8,128)(2,1)S(1)} async-done(((bf16[32,32,128]{2,1,0:T(8,128)(2,1)}), bf16[32,32,128]{2,1,0:T(8,128)(2,1)S(1)}, u32[]{:S(2)}, u32[]{:S(2)}) %all-to-all-start) | async-done | bytes 262176 | tf_op jit(solution)/shard_map/all_to_all | solution.py:595
  28.3 0.0 copy-done
  28.3 0.0 copy-done.1
  28.4 1.8 %shard_map.122 = (bf16[512,512]{1,0:T(8,128)(2,1)S(1)}, f32[16,8,128]{2,1,0:T(8,128)S(1)}) custom-call(f32[136,128]{1,0:T(8,128)S(1)} %get-tuple-element.18.table_ref, bf16[32,32,128]{2,1,0:T(8,128)(2,1)S(1)} %all-to-all-done.got_ref, f32[4,512,128]{2,1,0:T(8,128)S(1)} %get-tuple-element.19.conv_ref, bf16[512,512]{1,0:T(8,128)(2,1)S(1)} %copy-done, ...), custom_call_target="tpu_custom_call" | custom-call | flops 7864320 | bytes 983040 | tf_op jit(solution)/shard_map/pallas_call | solution.py:539
  30.1 14.9 %all_to_all.15.sums_ref = f32[16,8,128]{2,1,0:T(8,128)S(1)} all-to-all(f32[16,8,128]{2,1,0:T(8,128)S(1)} %get-tuple-element.20), channel_id=1, replica_groups=mesh['seq'=32,'chan'=16] {'chan'}, dimensions={0} | all-to-all | bytes 131072 | tf_op jit(solution)/shard_map/all_to_all | solution.py:610
  45.0 2.0 %shard_map.123 = (bf16[512,512]{1,0:T(8,128)(2,1)S(1)}, bf16[32,32,128]{2,1,0:T(8,128)(2,1)}, f32[8,128]{1,0:T(8,128)S(1)}) custom-call(f32[136,128]{1,0:T(8,128)S(1)} %get-tuple-element.18.table_ref, f32[16,8,128]{2,1,0:T(8,128)S(1)} %all_to_all.15.sums_ref, bf16[512,512]{1,0:T(8,128)(2,1)S(1)} %copy-done, bf16[512,512]{1,0:T(8,128)(2,1)S(1)} %copy-done.1, ...), custom_call_target="tpu_custom_call" | custom-call | flops 7864320 | bytes 983040 | tf_op jit(solution)/shard_map/pallas_call | solution.py:539
  47.0 4.6 %all-to-all-start.2 = ((bf16[32,32,128]{2,1,0:T(8,128)(2,1)}), bf16[32,32,128]{2,1,0:T(8,128)(2,1)S(1)}, u32[]{:S(2)}, u32[]{:S(2)}) async-start(bf16[32,32,128]{2,1,0:T(8,128)(2,1)} %get-tuple-element.28), calls=%async_computation.2 | async-start | bytes 524288 | tf_op jit(solution)/shard_map/all_to_all | solution.py:618
  51.6 1.6 %shard_map.124 = (bf16[512,512]{1,0:T(8,128)(2,1)}, bf16[512,512]{1,0:T(8,128)(2,1)}, f32[8,128]{1,0:T(8,128)S(1)}) custom-call(f32[136,128]{1,0:T(8,128)S(1)} %get-tuple-element.18.table_ref, f32[8,128]{1,0:T(8,128)S(1)} %get-tuple-element.22.totals_ref, bf16[512,512]{1,0:T(8,128)(2,1)S(1)} %copy-done, bf16[512,512]{1,0:T(8,128)(2,1)S(1)} %copy-done.1, ...), custom_call_target="tpu_custom_call" | custom-call | flops 5242880 | bytes 655360 | tf_op jit(solution)/shard_map/pallas_call | solution.py:539
  53.1 3.0 %shard_map.125 = (f32[4,512,128]{2,1,0:T(8,128)S(1)}, f32[64,128]{1,0:T(8,128)S(1)}) custom-call(s32[256]{0:T(256)S(1)} %copy-done.6, f32[136,128]{1,0:T(8,128)S(1)} %get-tuple-element.18.table_ref, bf16[512,512]{1,0:T(8,128)(2,1)S(1)} %get-tuple-element.25.adjoint_ref, f32[8,128]{1,0:T(8,128)S(1)} %get-tuple-element.26.done_ref), custom_call_target="tpu_custom_call" | custom-call | flops 13107200 | bytes 1638400 | tf_op jit(solution)/shard_map/pallas_call | solution.py:539
  56.1 0.0 copy-start.4
  56.2 1.0 %copy-done.4 = f32[4,512,128]{2,1,0:T(8,128)} copy-done((f32[4,512,128]{2,1,0:T(8,128)}, f32[4,512,128]{2,1,0:T(8,128)S(1)}, u32[]{:S(2)}) %copy-start.4) | copy-done | bytes 1048600
  57.1 7.2 %all-to-all-done.2.got_ref = bf16[32,32,128]{2,1,0:T(8,128)(2,1)S(1)} async-done(((bf16[32,32,128]{2,1,0:T(8,128)(2,1)}), bf16[32,32,128]{2,1,0:T(8,128)(2,1)S(1)}, u32[]{:S(2)}, u32[]{:S(2)}) %all-to-all-start.2) | async-done | bytes 262176 | tf_op jit(solution)/shard_map/all_to_all | solution.py:618
  64.4 2.7 %shard_map.126 = (bf16[512,512]{1,0:T(8,128)(2,1)}, bf16[512,512]{1,0:T(8,128)(2,1)}) custom-call(f32[136,128]{1,0:T(8,128)S(1)} %get-tuple-element.18.table_ref, f32[64,128]{1,0:T(8,128)S(1)} %get-tuple-element.27.flags_ref, bf16[32,32,128]{2,1,0:T(8,128)(2,1)S(1)} %all-to-all-done.2.got_ref, f32[4,512,128]{2,1,0:T(8,128)} %copy-done.4, ...), custom_call_target="tpu_custom_call" | custom-call | flops 7864320 | bytes 983040 | tf_op jit(solution)/shard_map/pallas_call | solution.py:539
  (1 shorter events, 0.0 us)
Async XLA Ops:
  0.6 15.4 %copy-start.5 = (f32[8,512]{1,0:T(8,128)S(1)}, f32[8,512]{1,0:T(8,128)}, u32[]{:S(2)}) copy-start(f32[8,512]{1,0:T(8,128)} %rate_hbm.1) | copy-start | bytes 49156
  0.6 15.4 %copy-start.9 = (f32[8,512]{1,0:T(8,128)S(1)}, f32[8,512]{1,0:T(8,128)}, u32[]{:S(2)}) copy-start(f32[8,512]{1,0:T(8,128)} %param.13) | copy-start | bytes 49156
  0.7 15.5 %copy-start.3 = (bf16[512,512]{1,0:T(8,128)(2,1)S(1)}, bf16[512,512]{1,0:T(8,128)(2,1)}, u32[]{:S(2)}) copy-start(bf16[512,512]{1,0:T(8,128)(2,1)} %value_hbm.3) | copy-start | bytes 1572868
  3.3 12.8 %copy-start.2 = (bf16[512,512]{1,0:T(8,128)(2,1)S(1)}, bf16[512,512]{1,0:T(8,128)(2,1)}, u32[]{:S(2)}) copy-start(bf16[512,512]{1,0:T(8,128)(2,1)} %key_hbm.3) | copy-start | bytes 1572868
  3.3 25.0 %all-to-all-start = ((bf16[32,32,128]{2,1,0:T(8,128)(2,1)}), bf16[32,32,128]{2,1,0:T(8,128)(2,1)S(1)}, u32[]{:S(2)}, u32[]{:S(2)}) async-start(bf16[32,32,128]{2,1,0:T(8,128)(2,1)} %shard_map.121), calls=%async_computation | async-start | bytes 524288 | tf_op jit(solution)/shard_map/all_to_all | solution.py:595
  16.1 0.7 %copy-start.8 = (f32[512]{0:T(512)S(1)}, f32[512]{0:T(512)}, u32[]{:S(2)}) copy-start(f32[512]{0:T(512)} %param.14) | copy-start | bytes 6148
  16.1 0.7 %copy-start.7 = (f32[512]{0:T(512)S(1)}, f32[512]{0:T(512)}, u32[]{:S(2)}) copy-start(f32[512]{0:T(512)} %param.15) | copy-start | bytes 6148
  16.1 0.7 %copy-start.6 = (s32[256]{0:T(256)S(1)}, s32[256]{0:T(256)}, u32[]{:S(2)}) copy-start(s32[256]{0:T(256)} %starts_ref.3) | copy-start | bytes 3076
  16.8 11.5 %copy-start = (bf16[512,512]{1,0:T(8,128)(2,1)S(1)}, bf16[512,512]{1,0:T(8,128)(2,1)}, u32[]{:S(2)}) copy-start(bf16[512,512]{1,0:T(8,128)(2,1)} %query_ref.5) | copy-start | bytes 1572868
  16.8 11.5 %copy-start.1 = (bf16[512,512]{1,0:T(8,128)(2,1)S(1)}, bf16[512,512]{1,0:T(8,128)(2,1)}, u32[]{:S(2)}) copy-start(bf16[512,512]{1,0:T(8,128)(2,1)} %cot_ref.5) | copy-start | bytes 1572868
  47.0 17.4 %all-to-all-start.2 = ((bf16[32,32,128]{2,1,0:T(8,128)(2,1)}), bf16[32,32,128]{2,1,0:T(8,128)(2,1)S(1)}, u32[]{:S(2)}, u32[]{:S(2)}) async-start(bf16[32,32,128]{2,1,0:T(8,128)(2,1)} %get-tuple-element.28), calls=%async_computation.2 | async-start | bytes 524288 | tf_op jit(solution)/shard_map/all_to_all | solution.py:618
  56.1 1.0 %copy-start.4 = (f32[4,512,128]{2,1,0:T(8,128)}, f32[4,512,128]{2,1,0:T(8,128)S(1)}, u32[]{:S(2)}) copy-start(f32[4,512,128]{2,1,0:T(8,128)S(1)} %get-tuple-element.29.conv_hbm) | copy-start | bytes 3145732

commit v2 on v1

--- a/solution.py
+++ b/solution.py
@@ -20,10 +20,10 @@
 GAIN, SKIP = 16, 17
 F32 = jnp.float32
 BF16 = jnp.bfloat16
-HIGHEST = lax.Precision.HIGHEST
 SEND = BF16
 UNROLL = 16
 LAG = 1
+HEAD = 2
 
 
 def rounded(array):
@@ -143,7 +143,7 @@
                 states = tuple(s * alive for s in states)
             for step in range(0, TILE, PAIR):
                 rows = slice(tile * TILE + step, tile * TILE + step + PAIR)
-                x = rounded(key_ref[group, rows, :].astype(F32) * value_ref[group, rows, :].astype(F32))
+                x = (key_ref[group, rows, :] * value_ref[group, rows, :]).astype(F32)
                 states = advance(factors, states, x[:ROWS])
                 states = advance(factors, states, x[ROWS:])
         fulls.append(gather_phases(states, powers))
@@ -206,7 +206,7 @@
 
     over_tile(step, tuple(work_ref[group, rows(TILE + m), :] for m in range(MODES)), reverse)
     for tile in range(tiles):
-        conv_ref[group, tile * TILE : (tile + 1) * TILE, :] = work_ref[group, tile_rows(tile), :]
+        conv_ref[tile * TILE : (tile + 1) * TILE, :] = work_ref[group, tile_rows(tile), :]
 
 
 def table_rows(tiles, groups, parts):
@@ -271,7 +271,7 @@
         lanes = lane_group(group)
         put_tiles(data_ref, group, rounded(key_ref[:, lanes].astype(F32) * value_ref[:, lanes].astype(F32)))
         rate, weight, skip = rate_ref[:, lanes], weight_ref[:, lanes], skip_ref[:, lanes]
-        local_conv(me, starts_ref, rate, weight, skip, data_ref, work_ref, conv_ref, group, False)
+        local_conv(me, starts_ref, rate, weight, skip, data_ref, work_ref, conv_ref.at[group], group, False)
         table_ref[table.rows(group, 0, MODES), :] = rate
         table_ref[table.rows(group, MODES, MODES), :] = weight
         table_ref[table.rows(group, GAIN, 1), :] = gain_ref[:, lanes]
@@ -282,17 +282,9 @@
         put_flag(table_ref, table.parts + part, keeps(starts_ref, part * tiles, tiles))
 
 
-def token_sums(array):
-    return [
-        lax.dot_general(
-            jnp.ones((ROWS, LANES), F32),
-            array[lane_group(block)],
-            (((1,), (1,)), ((), ())),
-            precision=HIGHEST,
-            preferred_element_type=F32,
-        )
-        for block in range(array.shape[0] // LANES)
-    ]
+def put_sums(sums, lane, array):
+    lanes = lax.broadcasted_iota(jnp.int32, (ROWS, LANES), 1)
+    return jnp.where(lanes == lane, jnp.sum(array, axis=1, keepdims=True), sums)
 
 
 def part_of(got_ref, part, groups):
@@ -316,6 +308,7 @@
     parts = got_ref.shape[0]
     me = lax.axis_index("seq")
     rates = [table.rate(group) for group in range(groups)]
+    sums = jnp.zeros((ROWS, LANES), F32)
     part_decay = [jnp.exp(-rate * tokens) for rate in rates]
     states = [jnp.zeros((MODES, LANES), F32)] * groups
     for part in range(parts - 1):
@@ -345,27 +338,27 @@
                 inner = cot_ref[rows, lanes].astype(F32) * gain * gated
                 if group:
                     square, inner = square + square_ref[rows, :], inner + inner_ref[rows, :]
-                square_ref[rows, :] = square
-                inner_ref[rows, :] = inner
-    sums = token_sums(square_ref[...]) + token_sums(inner_ref[...])
-    row = lax.broadcasted_iota(jnp.int32, (ROWS, LANES), 0)
-    block = sums[0]
-    for index in range(1, len(sums)):
-        block = jnp.where(row == index, sums[index], block)
+                if group < groups - 1:
+                    square_ref[rows, :] = square
+                    inner_ref[rows, :] = inner
+                    continue
+                for half in range(2):
+                    lane, part = (tile * TILE + step) // ROWS + half, slice(half * ROWS, (half + 1) * ROWS)
+                    sums = put_sums(sums, lane, square[part])
+                    sums = put_sums(sums, lane + LANES // 2, inner[part])
     for other in range(sums_ref.shape[0]):
-        sums_ref[other] = block
-
-
-def spread_sums(sums, scale_ref, shift_ref):
-    blocks = scale_ref.shape[0] // LANES
-    rinv = lax.rsqrt(sums / D + 1e-05)
-    lean = jnp.concatenate([sums[blocks:], sums[:blocks]], axis=0)
-    lean = rinv * rinv * rinv * lean / D
-    rinv, lean = jnp.transpose(rinv), jnp.transpose(lean)
-    for block in range(blocks):
-        rows = lane_group(block)
-        scale_ref[rows, :] = jnp.broadcast_to(rinv[:, block : block + 1], (LANES, LANES))
-        shift_ref[rows, :] = jnp.broadcast_to(lean[:, block : block + 1], (LANES, LANES))
+        sums_ref[other] = sums
+
+
+def norm_factors(sums):
+    half = LANES // 2
+    square, inner = sums[:, :half], sums[:, half:]
+    rinv = lax.rsqrt(square / D + 1e-05)
+    return rinv, rinv * rinv * rinv * inner / D
+
+
+def spread(array, lane):
+    return jnp.broadcast_to(array[:, lane : lane + 1], (ROWS, LANES))
 
 
 def backward_kernel(
@@ -385,7 +378,7 @@
     table = Table(table_ref, tiles, groups)
     sums = total(sums_ref[other] for other in range(sums_ref.shape[0]))
     totals_ref[...] = sums
-    spread_sums(sums, scale_ref, shift_ref)
+    rinv, lean = norm_factors(sums)
     fulls = []
     for group in range(groups):
         lanes = lane_group(group)
@@ -401,6 +394,11 @@
             for step in reversed(range(0, TILE, PAIR)):
                 rows = slice(tile * TILE + step, tile * TILE + step + PAIR)
                 query = query_ref[rows, lanes].astype(F32)
+                if group == 0:
+                    for half in range(2):
+                        lane, part = (tile * TILE + step) // ROWS + half, pl.ds(rows.start + half * ROWS, ROWS)
+                        scale_ref[part, :] = spread(rinv, lane)
+                        shift_ref[part, :] = spread(lean, lane)
                 gated = query * mixer_ref[rows, lanes].astype(F32)
                 scaled = cot_ref[rows, lanes].astype(F32) * gain
                 adjoint = ((scale_ref[rows, :] * scaled - gated * shift_ref[rows, :]) * query).astype(BF16)
@@ -418,7 +416,11 @@
     tokens, width = query_ref.shape
     tiles, groups = tokens // TILE, width // LANES
     table = Table(table_ref, tiles, groups)
-    spread_sums(totals_ref[...], scale_ref, shift_ref)
+    rinv, lean = norm_factors(totals_ref[...])
+    for lane in range(tokens // ROWS):
+        rows = slice(lane * ROWS, (lane + 1) * ROWS)
+        scale_ref[rows, :] = spread(rinv, lane)
+        shift_ref[rows, :] = spread(lean, lane)
     for group in range(groups):
         lanes = lane_group(group)
         gain = jnp.broadcast_to(table.gain(group), (TILE, LANES))
@@ -434,7 +436,7 @@
 
 
 def backward_local_kernel(
-    starts_ref, table_ref, adjoint_ref, done_ref, conv_ref, flags_ref, data_ref, work_ref
+    starts_ref, table_ref, adjoint_ref, done_ref, head_ref, tail_ref, flags_ref, data_ref, work_ref
 ):
     tokens, width = adjoint_ref.shape
     tiles, groups = tokens // TILE, width // LANES
@@ -442,10 +444,11 @@
     table = Table(table_ref, tiles, groups)
     for group in range(groups):
         put_tiles(data_ref, group, adjoint_ref[:, lane_group(group)].astype(F32))
+        conv = head_ref.at[group] if group < HEAD else tail_ref.at[group - HEAD]
         rate, weight, skip = table.rate(group), table.weight(group), table.skip(group)
-        local_conv(me, starts_ref, rate, weight, skip, data_ref, work_ref, conv_ref, group, True)
+        local_conv(me, starts_ref, rate, weight, skip, data_ref, work_ref, conv, group, True)
     for part in range(starts_ref.shape[0] // tiles):
-        put_flag(flags_ref, 2 * part, keeps(starts_ref, part * tiles + 1, tiles - 1))
+        put_flag(flags_ref, 2 * part, keeps(starts_ref, part * tiles, tiles))
         put_flag(flags_ref, 2 * part + 1, survive(starts_ref, part * tiles))
 
 
@@ -453,12 +456,13 @@
     table_ref,
     flags_ref,
     got_ref,
-    conv_hbm,
+    head_ref,
+    tail_hbm,
     key_hbm,
     value_hbm,
     grad_key_hbm,
     grad_value_hbm,
-    conv_ref,
+    tail_ref,
     key_ref,
     value_ref,
     dproduct_ref,
@@ -472,7 +476,7 @@
     parts = got_ref.shape[0]
     me = lax.axis_index("seq")
     copies = Copies(sems)
-    near = [copies.start(conv_hbm.at[group], conv_ref.at[group]) for group in range(groups)]
+    near = [copies.start(tail_hbm.at[group], tail_ref.at[group]) for group in range(groups - HEAD)]
     large = []
     for group in range(groups):
         lanes = lane_group(group)
@@ -486,10 +490,10 @@
     part_decay = [jnp.exp(-rate * tokens) for rate in rates]
     states = [jnp.zeros((MODES, LANES), F32)] * groups
     for part in range(parts - 1, 0, -1):
-        inner, alive = get_flag(flags_ref, 2 * part), get_flag(flags_ref, 2 * part + 1)
+        kept, alive = get_flag(flags_ref, 2 * part), get_flag(flags_ref, 2 * part + 1)
         arrived = part_of(got_ref, part, groups)
         states = [
-            jnp.where(part > me, (a + d * inner * s) * alive, s)
+            jnp.where(part > me, a * alive + d * kept * s, s)
             for a, d, s in zip(arrived, part_decay, states)
         ]
     out = []
@@ -498,17 +502,18 @@
         lanes = lane_group(group)
         for copy in large[group]:
             copy.wait()
-        dproduct = dproduct_ref[group].astype(F32)
-        grad_key_ref[group] = (dproduct * value_ref[group].astype(F32)).astype(BF16)
+        grad_key_ref[group] = dproduct_ref[group] * value_ref[group]
         out.append(copies.start(grad_key_ref.at[group], grad_key_hbm.at[:, lanes]))
-        grad_value_ref[group] = (dproduct * key_ref[group].astype(F32)).astype(BF16)
+        grad_value_ref[group] = dproduct_ref[group] * key_ref[group]
         out.append(copies.start(grad_value_ref.at[group], grad_value_hbm.at[:, lanes]))
 
     for group in range(groups):
         lanes = lane_group(group)
         factors = per_mode(jnp.exp(-rates[group] * ROWS))
         carry = weighted(phase_powers(rates[group], ROWS, -1), states[group] * table.weight(group))
-        near[group].wait()
+        if group >= HEAD:
+            near[group - HEAD].wait()
+        conv = head_ref.at[group] if group < HEAD else tail_ref.at[group - HEAD]
         for tile in reversed(range(tiles)):
             if tile < tiles - 1:
                 alive = table.alive(tile + 1)
@@ -519,7 +524,7 @@
                 for _ in range(2):
                     extra.append(total(carry))
                     carry = [c * f for c, f in zip(carry, factors)]
-                dproduct = conv_ref[group, rows, :] + jnp.concatenate(extra[::-1], axis=0)
+                dproduct = conv[rows, :] + jnp.concatenate(extra[::-1], axis=0)
                 dproduct_ref[group, rows, :] = dproduct.astype(BF16)
         if group >= LAG:
             finish(group - LAG)
@@ -567,6 +572,7 @@
     whole, split, pitched = (tokens, width), (groups, tokens, LANES), (groups, tiles * PITCH, LANES)
     block, spread, summed = (parts, groups * MODES, LANES), (tokens, LANES), (peers, ROWS, LANES)
     modes, packed = (MODES, width), (table_rows(tiles, groups, parts), LANES)
+    head_split, tail_split = (HEAD, tokens, LANES), (groups - HEAD, tokens, LANES)
     work = tokens * width
 
     def vmem(*arrays):
@@ -623,18 +629,18 @@
         [spread, spread],
         work * 20,
     )
-    conv, flags = call(
+    head, tail, flags = call(
         backward_local_kernel,
         [starts] + vmem(table, adjoint, done),
-        [(split, F32), ((2 * parts, LANES), F32)],
+        [(head_split, F32), (tail_split, F32), ((2 * parts, LANES), F32)],
         [pitched, pitched],
         work * 50,
     )
     grad_key, grad_value = call(
         backward_join_kernel,
-        vmem(table, flags, got) + hbm(conv, key_feat, value_feat),
+        vmem(table, flags, got, head) + hbm(tail, key_feat, value_feat),
         [(whole, BF16, pl.ANY), (whole, BF16, pl.ANY)],
-        [split] + [(split, BF16)] * 5 + [sems(5 * groups)],
+        [tail_split] + [(split, BF16)] * 5 + [sems(5 * groups - HEAD)],
         work * 30,
         53,
     )

time: 67.5 us -> 66.5 us (0.985)
  Pallas kernels: 16.7 us -> 15.7 us
    pallas_call x7, Pallas kernels: 16.7 us -> 15.7 us  [call(): pl.pallas_call(kernel, out_shape=[jax.ShapeDtypeStruct(*out[:2]) for out...]
where the time goes in v2:
time: 66.5 us; the launch traced here: 66.1 us
  starting transfers between devices  17.3 us (26%)
  waiting for transfers between devices  16 us (24%)
  Pallas kernels  15.7 us (24%)
  blocking collectives  14.9 us (22%)
  local copies, waits for them, and re-layouts  1.49 us (2%)
  between operations  0.78 us (1%)
    all_to_all x2, starting transfers between devices, on_device(): got = lax.all_to_all(send, 'seq', 0, 0)  17.3 us
    all_to_all x2, waiting for transfers between devices, on_device(): got = lax.all_to_all(send, 'seq', 0, 0)  16 us
    pallas_call x7, Pallas kernels, call(): pl.pallas_call(kernel, out_shape=[jax.ShapeDtypeStruct(*out[:2]) for out...  15.7 us
    all_to_all x1, blocking collectives, on_device(): sums = lax.all_to_all(sums, 'chan', 0, 0)  14.9 us
    unnamed x20, local copies, waits for them, and re-layouts  1.49 us
  transfers between devices with their start and end apart: 2, of which 2 were waited for; matrix products, arithmetic and copies ran while one was open for 0% of the time, Pallas kernels for 11%

profile of v2, /device:TPU:64, one launch (start us, length us, event | category | flops | bytes accessed | tf_op | source)
XLA Modules:
  0.0 66.1 jit_solution(3093445512176531894)
XLA Ops:
  0.6 0.0 copy-start.5
  0.6 0.0 copy-start.9
  0.7 0.0 copy-start.3
  0.7 2.6 %shard_map.121 = bf16[32,32,128]{2,1,0:T(8,128)(2,1)} custom-call(s32[256]{0:T(256)} %starts_ref.3, bf16[512,512]{1,0:T(8,128)(2,1)} %key_hbm.3, bf16[512,512]{1,0:T(8,128)(2,1)} %value_hbm.3, f32[8,512]{1,0:T(8,128)} %rate_hbm.1), custom_call_target="tpu_custom_call" | custom-call | flops 5242880 | bytes 655360 | tf_op jit(solution)/shard_map/pallas_call | solution.py:544
  3.2 0.0 copy-start.2
  3.2 12.7 %all-to-all-start = ((bf16[32,32,128]{2,1,0:T(8,128)(2,1)}), bf16[32,32,128]{2,1,0:T(8,128)(2,1)S(1)}, u32[]{:S(2)}, u32[]{:S(2)}) async-start(bf16[32,32,128]{2,1,0:T(8,128)(2,1)} %shard_map.121), calls=%async_computation | async-start | bytes 524288 | tf_op jit(solution)/shard_map/all_to_all | solution.py:601
  16.0 0.0 copy-done.5
  16.0 0.0 copy-done.9
  16.0 0.0 copy-start.8
  16.0 0.0 copy-start.7
  16.1 0.0 copy-start.6
  16.1 0.0 copy-done.3
  16.1 0.0 copy-done.2
  16.1 0.6 copy-done.8
  16.7 0.0 copy-done.7
  16.7 0.0 copy-done.6
  16.7 0.0 copy-start
  16.7 0.0 copy-start.1
  16.7 3.0 %shard_map.120 = (f32[4,512,128]{2,1,0:T(8,128)S(1)}, f32[136,128]{1,0:T(8,128)S(1)}) custom-call(s32[256]{0:T(256)S(1)} %copy-done.6, bf16[512,512]{1,0:T(8,128)(2,1)S(1)} %copy-done.2, bf16[512,512]{1,0:T(8,128)(2,1)S(1)} %copy-done.3, f32[8,512]{1,0:T(8,128)S(1)} %copy-done.5, f32[8,512]{1,0:T(8,128)S(1)} %sqrt_multiply_fusion.weight_ref, ...), custom_call_target="tpu_custom_call" | custom-call | flops 13107200 | bytes 1638400 | tf_op jit(solution)/shard_map/pallas_call | solution.py:544
  19.8 8.5 %all-to-all-done.got_ref = bf16[32,32,128]{2,1,0:T(8,128)(2,1)S(1)} async-done(((bf16[32,32,128]{2,1,0:T(8,128)(2,1)}), bf16[32,32,128]{2,1,0:T(8,128)(2,1)S(1)}, u32[]{:S(2)}, u32[]{:S(2)}) %all-to-all-start) | async-done | bytes 262176 | tf_op jit(solution)/shard_map/all_to_all | solution.py:601
  28.3 0.0 copy-done
  28.3 0.0 copy-done.1
  28.3 1.2 %shard_map.122 = (bf16[512,512]{1,0:T(8,128)(2,1)S(1)}, f32[16,8,128]{2,1,0:T(8,128)S(1)}) custom-call(f32[136,128]{1,0:T(8,128)S(1)} %get-tuple-element.19.table_ref, bf16[32,32,128]{2,1,0:T(8,128)(2,1)S(1)} %all-to-all-done.got_ref, f32[4,512,128]{2,1,0:T(8,128)S(1)} %get-tuple-element.20.conv_ref, bf16[512,512]{1,0:T(8,128)(2,1)S(1)} %copy-done, ...), custom_call_target="tpu_custom_call" | custom-call | flops 7864320 | bytes 983040 | tf_op jit(solution)/shard_map/pallas_call | solution.py:544
  29.4 14.9 %all_to_all.15.sums_ref = f32[16,8,128]{2,1,0:T(8,128)S(1)} all-to-all(f32[16,8,128]{2,1,0:T(8,128)S(1)} %get-tuple-element.21), channel_id=1, replica_groups=mesh['seq'=32,'chan'=16] {'chan'}, dimensions={0} | all-to-all | bytes 131072 | tf_op jit(solution)/shard_map/all_to_all | solution.py:616
  44.3 1.9 %shard_map.123 = (bf16[512,512]{1,0:T(8,128)(2,1)S(1)}, bf16[32,32,128]{2,1,0:T(8,128)(2,1)}, f32[8,128]{1,0:T(8,128)S(1)}) custom-call(f32[136,128]{1,0:T(8,128)S(1)} %get-tuple-element.19.table_ref, f32[16,8,128]{2,1,0:T(8,128)S(1)} %all_to_all.15.sums_ref, bf16[512,512]{1,0:T(8,128)(2,1)S(1)} %copy-done, bf16[512,512]{1,0:T(8,128)(2,1)S(1)} %copy-done.1, ...), custom_call_target="tpu_custom_call" | custom-call | flops 7864320 | bytes 983040 | tf_op jit(solution)/shard_map/pallas_call | solution.py:544
  46.2 4.6 %all-to-all-start.2 = ((bf16[32,32,128]{2,1,0:T(8,128)(2,1)}), bf16[32,32,128]{2,1,0:T(8,128)(2,1)S(1)}, u32[]{:S(2)}, u32[]{:S(2)}) async-start(bf16[32,32,128]{2,1,0:T(8,128)(2,1)} %get-tuple-element.29), calls=%async_computation.2 | async-start | bytes 524288 | tf_op jit(solution)/shard_map/all_to_all | solution.py:624
  50.8 1.5 %shard_map.124 = (bf16[512,512]{1,0:T(8,128)(2,1)}, bf16[512,512]{1,0:T(8,128)(2,1)}, f32[8,128]{1,0:T(8,128)S(1)}) custom-call(f32[136,128]{1,0:T(8,128)S(1)} %get-tuple-element.19.table_ref, f32[8,128]{1,0:T(8,128)S(1)} %get-tuple-element.23.totals_ref, bf16[512,512]{1,0:T(8,128)(2,1)S(1)} %copy-done, bf16[512,512]{1,0:T(8,128)(2,1)S(1)} %copy-done.1, ...), custom_call_target="tpu_custom_call" | custom-call | flops 5242880 | bytes 655360 | tf_op jit(solution)/shard_map/pallas_call | solution.py:544
  52.3 3.0 %shard_map.125 = (f32[2,512,128]{2,1,0:T(8,128)S(1)}, f32[2,512,128]{2,1,0:T(8,128)S(1)}, f32[64,128]{1,0:T(8,128)S(1)}) custom-call(s32[256]{0:T(256)S(1)} %copy-done.6, f32[136,128]{1,0:T(8,128)S(1)} %get-tuple-element.19.table_ref, bf16[512,512]{1,0:T(8,128)(2,1)S(1)} %get-tuple-element.26.adjoint_ref, f32[8,128]{1,0:T(8,128)S(1)} %get-tuple-element.27.done_ref), custom_call_target="tpu_custom_call" | custom-call | flops 13107200 | bytes 1638400 | tf_op jit(solution)/shard_map/pallas_call | solution.py:544
  55.3 0.0 copy-start.4
  55.3 0.8 %copy-done.4 = f32[2,512,128]{2,1,0:T(8,128)} copy-done((f32[2,512,128]{2,1,0:T(8,128)}, f32[2,512,128]{2,1,0:T(8,128)S(1)}, u32[]{:S(2)}) %copy-start.4) | copy-done | bytes 524312
  56.1 7.5 %all-to-all-done.2.got_ref = bf16[32,32,128]{2,1,0:T(8,128)(2,1)S(1)} async-done(((bf16[32,32,128]{2,1,0:T(8,128)(2,1)}), bf16[32,32,128]{2,1,0:T(8,128)(2,1)S(1)}, u32[]{:S(2)}, u32[]{:S(2)}) %all-to-all-start.2) | async-done | bytes 262176 | tf_op jit(solution)/shard_map/all_to_all | solution.py:624
  63.6 2.5 %shard_map.126 = (bf16[512,512]{1,0:T(8,128)(2,1)}, bf16[512,512]{1,0:T(8,128)(2,1)}) custom-call(f32[136,128]{1,0:T(8,128)S(1)} %get-tuple-element.19.table_ref, f32[64,128]{1,0:T(8,128)S(1)} %get-tuple-element.28.flags_ref, bf16[32,32,128]{2,1,0:T(8,128)(2,1)S(1)} %all-to-all-done.2.got_ref, f32[2,512,128]{2,1,0:T(8,128)S(1)} %get-tuple-element.30.head_ref, ...), custom_call_target="tpu_custom_call" | custom-call | flops 7864320 | bytes 983040 | tf_op jit(solution)/shard_map/pallas_call | solution.py:544
  (1 shorter events, 0.0 us)
Async XLA Ops:
  0.6 15.3 %copy-start.5 = (f32[8,512]{1,0:T(8,128)S(1)}, f32[8,512]{1,0:T(8,128)}, u32[]{:S(2)}) copy-start(f32[8,512]{1,0:T(8,128)} %rate_hbm.1) | copy-start | bytes 49156
  0.6 15.3 %copy-start.9 = (f32[8,512]{1,0:T(8,128)S(1)}, f32[8,512]{1,0:T(8,128)}, u32[]{:S(2)}) copy-start(f32[8,512]{1,0:T(8,128)} %param.13) | copy-start | bytes 49156
  0.7 15.4 %copy-start.3 = (bf16[512,512]{1,0:T(8,128)(2,1)S(1)}, bf16[512,512]{1,0:T(8,128)(2,1)}, u32[]{:S(2)}) copy-start(bf16[512,512]{1,0:T(8,128)(2,1)} %value_hbm.3) | copy-start | bytes 1572868
  3.2 12.8 %copy-start.2 = (bf16[512,512]{1,0:T(8,128)(2,1)S(1)}, bf16[512,512]{1,0:T(8,128)(2,1)}, u32[]{:S(2)}) copy-start(bf16[512,512]{1,0:T(8,128)(2,1)} %key_hbm.3) | copy-start | bytes 1572868
  3.2 25.0 %all-to-all-start = ((bf16[32,32,128]{2,1,0:T(8,128)(2,1)}), bf16[32,32,128]{2,1,0:T(8,128)(2,1)S(1)}, u32[]{:S(2)}, u32[]{:S(2)}) async-start(bf16[32,32,128]{2,1,0:T(8,128)(2,1)} %shard_map.121), calls=%async_computation | async-start | bytes 524288 | tf_op jit(solution)/shard_map/all_to_all | solution.py:601
  16.0 0.7 %copy-start.8 = (f32[512]{0:T(512)S(1)}, f32[512]{0:T(512)}, u32[]{:S(2)}) copy-start(f32[512]{0:T(512)} %param.14) | copy-start | bytes 6148
  16.0 0.7 %copy-start.7 = (f32[512]{0:T(512)S(1)}, f32[512]{0:T(512)}, u32[]{:S(2)}) copy-start(f32[512]{0:T(512)} %param.15) | copy-start | bytes 6148
  16.1 0.7 %copy-start.6 = (s32[256]{0:T(256)S(1)}, s32[256]{0:T(256)}, u32[]{:S(2)}) copy-start(s32[256]{0:T(256)} %starts_ref.3) | copy-start | bytes 3076
  16.7 11.5 %copy-start = (bf16[512,512]{1,0:T(8,128)(2,1)S(1)}, bf16[512,512]{1,0:T(8,128)(2,1)}, u32[]{:S(2)}) copy-start(bf16[512,512]{1,0:T(8,128)(2,1)} %query_ref.5) | copy-start | bytes 1572868
  16.7 11.5 %copy-start.1 = (bf16[512,512]{1,0:T(8,128)(2,1)S(1)}, bf16[512,512]{1,0:T(8,128)(2,1)}, u32[]{:S(2)}) copy-start(bf16[512,512]{1,0:T(8,128)(2,1)} %cot_ref.5) | copy-start | bytes 1572868
  46.2 17.4 %all-to-all-start.2 = ((bf16[32,32,128]{2,1,0:T(8,128)(2,1)}), bf16[32,32,128]{2,1,0:T(8,128)(2,1)S(1)}, u32[]{:S(2)}, u32[]{:S(2)}) async-start(bf16[32,32,128]{2,1,0:T(8,128)(2,1)} %get-tuple-element.29), calls=%async_computation.2 | async-start | bytes 524288 | tf_op jit(solution)/shard_map/all_to_all | solution.py:624
  55.3 0.8 %copy-start.4 = (f32[2,512,128]{2,1,0:T(8,128)}, f32[2,512,128]{2,1,0:T(8,128)S(1)}, u32[]{:S(2)}) copy-start(f32[2,512,128]{2,1,0:T(8,128)S(1)} %get-tuple-element.31.tail_hbm) | copy-start | bytes 1572868

commit v3 on v2

--- a/solution.py
+++ b/solution.py
@@ -22,7 +22,7 @@
 BF16 = jnp.bfloat16
 SEND = BF16
 UNROLL = 16
-LAG = 1
+LAG = 3
 HEAD = 2
 
 
@@ -457,12 +457,11 @@
     flags_ref,
     got_ref,
     head_ref,
-    tail_hbm,
+    tail_ref,
     key_hbm,
     value_hbm,
     grad_key_hbm,
     grad_value_hbm,
-    tail_ref,
     key_ref,
     value_ref,
     dproduct_ref,
@@ -476,7 +475,6 @@
     parts = got_ref.shape[0]
     me = lax.axis_index("seq")
     copies = Copies(sems)
-    near = [copies.start(tail_hbm.at[group], tail_ref.at[group]) for group in range(groups - HEAD)]
     large = []
     for group in range(groups):
         lanes = lane_group(group)
@@ -511,8 +509,6 @@
         lanes = lane_group(group)
         factors = per_mode(jnp.exp(-rates[group] * ROWS))
         carry = weighted(phase_powers(rates[group], ROWS, -1), states[group] * table.weight(group))
-        if group >= HEAD:
-            near[group - HEAD].wait()
         conv = head_ref.at[group] if group < HEAD else tail_ref.at[group - HEAD]
         for tile in reversed(range(tiles)):
             if tile < tiles - 1:
@@ -638,11 +634,11 @@
     )
     grad_key, grad_value = call(
         backward_join_kernel,
-        vmem(table, flags, got, head) + hbm(tail, key_feat, value_feat),
+        vmem(table, flags, got, head, tail) + hbm(key_feat, value_feat),
         [(whole, BF16, pl.ANY), (whole, BF16, pl.ANY)],
-        [tail_split] + [(split, BF16)] * 5 + [sems(5 * groups - HEAD)],
+        [(split, BF16)] * 5 + [sems(4 * groups)],
         work * 30,
-        53,
+        52,
     )
     return mixed, grad_query, grad_key, grad_value
 

time: 66.5 us -> 66.1 us (level)
  waiting for transfers between devices: 16 us -> 16.8 us
  local copies, waits for them, and re-layouts: 1.49 us -> 0.69 us
    all_to_all x2, waiting for transfers between devices: 16 us -> 16.8 us  [on_device(): got = lax.all_to_all(send, 'seq', 0, 0)]
    unnamed x20 -> x18, local copies, waits for them, and re-layouts: 1.49 us -> 0.69 us
where the time goes in v3:
time: 66.1 us; the launch traced here: 65.7 us
  starting transfers between devices  17.3 us (26%)
  waiting for transfers between devices  16.8 us (25%)
  Pallas kernels  15.3 us (23%)
  blocking collectives  14.9 us (23%)
  between operations  0.77 us (1%)
  local copies, waits for them, and re-layouts  0.69 us (1%)
    all_to_all x2, starting transfers between devices, on_device(): got = lax.all_to_all(send, 'seq', 0, 0)  17.3 us
    all_to_all x2, waiting for transfers between devices, on_device(): got = lax.all_to_all(send, 'seq', 0, 0)  16.8 us
    pallas_call x7, Pallas kernels, call(): pl.pallas_call(kernel, out_shape=[jax.ShapeDtypeStruct(*out[:2]) for out...  15.3 us
    all_to_all x1, blocking collectives, on_device(): sums = lax.all_to_all(sums, 'chan', 0, 0)  14.9 us
  transfers between devices with their start and end apart: 2, of which 2 were waited for; matrix products, arithmetic and copies ran while one was open for 0% of the time, Pallas kernels for 11%

profile of v3, /device:TPU:64, one launch (start us, length us, event | category | flops | bytes accessed | tf_op | source)
XLA Modules:
  0.0 65.7 jit_solution(6777117899846929387)
XLA Ops:
  0.6 0.0 copy-start.4
  0.6 0.0 copy-start.8
  0.7 0.0 copy-start.3
  0.7 2.6 %shard_map.121 = bf16[32,32,128]{2,1,0:T(8,128)(2,1)} custom-call(s32[256]{0:T(256)} %starts_ref.3, bf16[512,512]{1,0:T(8,128)(2,1)} %key_hbm.3, bf16[512,512]{1,0:T(8,128)(2,1)} %value_hbm.3, f32[8,512]{1,0:T(8,128)} %rate_hbm.1), custom_call_target="tpu_custom_call" | custom-call | flops 5242880 | bytes 655360 | tf_op jit(solution)/shard_map/pallas_call | solution.py:540
  3.2 0.0 copy-start.2
  3.2 12.7 %all-to-all-start = ((bf16[32,32,128]{2,1,0:T(8,128)(2,1)}), bf16[32,32,128]{2,1,0:T(8,128)(2,1)S(1)}, u32[]{:S(2)}, u32[]{:S(2)}) async-start(bf16[32,32,128]{2,1,0:T(8,128)(2,1)} %shard_map.121), calls=%async_computation | async-start | bytes 524288 | tf_op jit(solution)/shard_map/all_to_all | solution.py:597
  16.0 0.0 copy-done.4
  16.0 0.0 copy-done.8
  16.0 0.0 copy-start.7
  16.0 0.0 copy-start.6
  16.1 0.0 copy-start.5
  16.1 0.0 copy-done.3
  16.1 0.0 copy-done.2
  16.1 0.6 copy-done.7
  16.7 0.0 copy-done.6
  16.7 0.0 copy-done.5
  16.7 0.0 copy-start
  16.7 0.0 copy-start.1
  16.7 3.0 %shard_map.120 = (f32[4,512,128]{2,1,0:T(8,128)S(1)}, f32[136,128]{1,0:T(8,128)S(1)}) custom-call(s32[256]{0:T(256)S(1)} %copy-done.5, bf16[512,512]{1,0:T(8,128)(2,1)S(1)} %copy-done.2, bf16[512,512]{1,0:T(8,128)(2,1)S(1)} %copy-done.3, f32[8,512]{1,0:T(8,128)S(1)} %copy-done.4, f32[8,512]{1,0:T(8,128)S(1)} %sqrt_multiply_fusion.weight_ref, ...), custom_call_target="tpu_custom_call" | custom-call | flops 13107200 | bytes 1638400 | tf_op jit(solution)/shard_map/pallas_call | solution.py:540
  19.8 8.5 %all-to-all-done.got_ref = bf16[32,32,128]{2,1,0:T(8,128)(2,1)S(1)} async-done(((bf16[32,32,128]{2,1,0:T(8,128)(2,1)}), bf16[32,32,128]{2,1,0:T(8,128)(2,1)S(1)}, u32[]{:S(2)}, u32[]{:S(2)}) %all-to-all-start) | async-done | bytes 262176 | tf_op jit(solution)/shard_map/all_to_all | solution.py:597
  28.3 0.0 copy-done
  28.3 0.0 copy-done.1
  28.3 1.2 %shard_map.122 = (bf16[512,512]{1,0:T(8,128)(2,1)S(1)}, f32[16,8,128]{2,1,0:T(8,128)S(1)}) custom-call(f32[136,128]{1,0:T(8,128)S(1)} %get-tuple-element.19.table_ref, bf16[32,32,128]{2,1,0:T(8,128)(2,1)S(1)} %all-to-all-done.got_ref, f32[4,512,128]{2,1,0:T(8,128)S(1)} %get-tuple-element.20.conv_ref, bf16[512,512]{1,0:T(8,128)(2,1)S(1)} %copy-done, ...), custom_call_target="tpu_custom_call" | custom-call | flops 7864320 | bytes 983040 | tf_op jit(solution)/shard_map/pallas_call | solution.py:540
  29.4 14.9 %all_to_all.15.sums_ref = f32[16,8,128]{2,1,0:T(8,128)S(1)} all-to-all(f32[16,8,128]{2,1,0:T(8,128)S(1)} %get-tuple-element.21), channel_id=1, replica_groups=mesh['seq'=32,'chan'=16] {'chan'}, dimensions={0} | all-to-all | bytes 131072 | tf_op jit(solution)/shard_map/all_to_all | solution.py:612
  44.3 1.9 %shard_map.123 = (bf16[512,512]{1,0:T(8,128)(2,1)S(1)}, bf16[32,32,128]{2,1,0:T(8,128)(2,1)}, f32[8,128]{1,0:T(8,128)S(1)}) custom-call(f32[136,128]{1,0:T(8,128)S(1)} %get-tuple-element.19.table_ref, f32[16,8,128]{2,1,0:T(8,128)S(1)} %all_to_all.15.sums_ref, bf16[512,512]{1,0:T(8,128)(2,1)S(1)} %copy-done, bf16[512,512]{1,0:T(8,128)(2,1)S(1)} %copy-done.1, ...), custom_call_target="tpu_custom_call" | custom-call | flops 7864320 | bytes 983040 | tf_op jit(solution)/shard_map/pallas_call | solution.py:540
  46.2 4.6 %all-to-all-start.2 = ((bf16[32,32,128]{2,1,0:T(8,128)(2,1)}), bf16[32,32,128]{2,1,0:T(8,128)(2,1)S(1)}, u32[]{:S(2)}, u32[]{:S(2)}) async-start(bf16[32,32,128]{2,1,0:T(8,128)(2,1)} %get-tuple-element.29), calls=%async_computation.2 | async-start | bytes 524288 | tf_op jit(solution)/shard_map/all_to_all | solution.py:620
  50.8 1.5 %shard_map.124 = (bf16[512,512]{1,0:T(8,128)(2,1)}, bf16[512,512]{1,0:T(8,128)(2,1)}, f32[8,128]{1,0:T(8,128)S(1)}) custom-call(f32[136,128]{1,0:T(8,128)S(1)} %get-tuple-element.19.table_ref, f32[8,128]{1,0:T(8,128)S(1)} %get-tuple-element.23.totals_ref, bf16[512,512]{1,0:T(8,128)(2,1)S(1)} %copy-done, bf16[512,512]{1,0:T(8,128)(2,1)S(1)} %copy-done.1, ...), custom_call_target="tpu_custom_call" | custom-call | flops 5242880 | bytes 655360 | tf_op jit(solution)/shard_map/pallas_call | solution.py:540
  52.3 3.0 %shard_map.125 = (f32[2,512,128]{2,1,0:T(8,128)S(1)}, f32[2,512,128]{2,1,0:T(8,128)S(1)}, f32[64,128]{1,0:T(8,128)S(1)}) custom-call(s32[256]{0:T(256)S(1)} %copy-done.5, f32[136,128]{1,0:T(8,128)S(1)} %get-tuple-element.19.table_ref, bf16[512,512]{1,0:T(8,128)(2,1)S(1)} %get-tuple-element.26.adjoint_ref, f32[8,128]{1,0:T(8,128)S(1)} %get-tuple-element.27.done_ref), custom_call_target="tpu_custom_call" | custom-call | flops 13107200 | bytes 1638400 | tf_op jit(solution)/shard_map/pallas_call | solution.py:540
  55.3 8.3 %all-to-all-done.2.got_ref = bf16[32,32,128]{2,1,0:T(8,128)(2,1)S(1)} async-done(((bf16[32,32,128]{2,1,0:T(8,128)(2,1)}), bf16[32,32,128]{2,1,0:T(8,128)(2,1)S(1)}, u32[]{:S(2)}, u32[]{:S(2)}) %all-to-all-start.2) | async-done | bytes 262176 | tf_op jit(solution)/shard_map/all_to_all | solution.py:620
  63.6 2.1 %shard_map.126 = (bf16[512,512]{1,0:T(8,128)(2,1)}, bf16[512,512]{1,0:T(8,128)(2,1)}) custom-call(f32[136,128]{1,0:T(8,128)S(1)} %get-tuple-element.19.table_ref, f32[64,128]{1,0:T(8,128)S(1)} %get-tuple-element.28.flags_ref, bf16[32,32,128]{2,1,0:T(8,128)(2,1)S(1)} %all-to-all-done.2.got_ref, f32[2,512,128]{2,1,0:T(8,128)S(1)} %get-tuple-element.30.head_ref, ...), custom_call_target="tpu_custom_call" | custom-call | flops 7864320 | bytes 983040 | tf_op jit(solution)/shard_map/pallas_call | solution.py:540
  (1 shorter events, 0.0 us)
Async XLA Ops:
  0.6 15.3 %copy-start.4 = (f32[8,512]{1,0:T(8,128)S(1)}, f32[8,512]{1,0:T(8,128)}, u32[]{:S(2)}) copy-start(f32[8,512]{1,0:T(8,128)} %rate_hbm.1) | copy-start | bytes 49156
  0.6 15.3 %copy-start.8 = (f32[8,512]{1,0:T(8,128)S(1)}, f32[8,512]{1,0:T(8,128)}, u32[]{:S(2)}) copy-start(f32[8,512]{1,0:T(8,128)} %param.13) | copy-start | bytes 49156
  0.7 15.4 %copy-start.3 = (bf16[512,512]{1,0:T(8,128)(2,1)S(1)}, bf16[512,512]{1,0:T(8,128)(2,1)}, u32[]{:S(2)}) copy-start(bf16[512,512]{1,0:T(8,128)(2,1)} %value_hbm.3) | copy-start | bytes 1572868
  3.2 12.8 %copy-start.2 = (bf16[512,512]{1,0:T(8,128)(2,1)S(1)}, bf16[512,512]{1,0:T(8,128)(2,1)}, u32[]{:S(2)}) copy-start(bf16[512,512]{1,0:T(8,128)(2,1)} %key_hbm.3) | copy-start | bytes 1572868
  3.2 25.0 %all-to-all-start = ((bf16[32,32,128]{2,1,0:T(8,128)(2,1)}), bf16[32,32,128]{2,1,0:T(8,128)(2,1)S(1)}, u32[]{:S(2)}, u32[]{:S(2)}) async-start(bf16[32,32,128]{2,1,0:T(8,128)(2,1)} %shard_map.121), calls=%async_computation | async-start | bytes 524288 | tf_op jit(solution)/shard_map/all_to_all | solution.py:597
  16.0 0.7 %copy-start.7 = (f32[512]{0:T(512)S(1)}, f32[512]{0:T(512)}, u32[]{:S(2)}) copy-start(f32[512]{0:T(512)} %param.14) | copy-start | bytes 6148
  16.0 0.7 %copy-start.6 = (f32[512]{0:T(512)S(1)}, f32[512]{0:T(512)}, u32[]{:S(2)}) copy-start(f32[512]{0:T(512)} %param.15) | copy-start | bytes 6148
  16.1 0.7 %copy-start.5 = (s32[256]{0:T(256)S(1)}, s32[256]{0:T(256)}, u32[]{:S(2)}) copy-start(s32[256]{0:T(256)} %starts_ref.3) | copy-start | bytes 3076
  16.7 11.5 %copy-start = (bf16[512,512]{1,0:T(8,128)(2,1)S(1)}, bf16[512,512]{1,0:T(8,128)(2,1)}, u32[]{:S(2)}) copy-start(bf16[512,512]{1,0:T(8,128)(2,1)} %query_ref.5) | copy-start | bytes 1572868
  16.7 11.5 %copy-start.1 = (bf16[512,512]{1,0:T(8,128)(2,1)S(1)}, bf16[512,512]{1,0:T(8,128)(2,1)}, u32[]{:S(2)}) copy-start(bf16[512,512]{1,0:T(8,128)(2,1)} %cot_ref.5) | copy-start | bytes 1572868
  46.2 17.4 %all-to-all-start.2 = ((bf16[32,32,128]{2,1,0:T(8,128)(2,1)}), bf16[32,32,128]{2,1,0:T(8,128)(2,1)S(1)}, u32[]{:S(2)}, u32[]{:S(2)}) async-start(bf16[32,32,128]{2,1,0:T(8,128)(2,1)} %get-tuple-element.29), calls=%async_computation.2 | async-start | bytes 524288 | tf_op jit(solution)/shard_map/all_to_all | solution.py:620

commit v4 on v3

--- a/solution.py
+++ b/solution.py
@@ -288,7 +288,8 @@
 
 
 def part_of(got_ref, part, groups):
-    return [got_ref[part, rows_of(group), :].astype(F32) for group in range(groups)]
+    block = got_ref[part].astype(F32)
+    return [block[rows_of(group)] for group in range(groups)]
 
 
 def forward_join_kernel(

time: 66.1 us -> 66.1 us (level)
  no operation moved by 1% of the time
where the time goes in v4:
time: 66.1 us; the launch traced here: 65.7 us
  starting transfers between devices  17.3 us (26%)
  waiting for transfers between devices  16.8 us (25%)
  Pallas kernels  15.3 us (23%)
  blocking collectives  14.9 us (23%)
  between operations  0.77 us (1%)
  local copies, waits for them, and re-layouts  0.69 us (1%)
    all_to_all x2, starting transfers between devices, on_device(): got = lax.all_to_all(send, 'seq', 0, 0)  17.3 us
    all_to_all x2, waiting for transfers between devices, on_device(): got = lax.all_to_all(send, 'seq', 0, 0)  16.8 us
    pallas_call x7, Pallas kernels, call(): pl.pallas_call(kernel, out_shape=[jax.ShapeDtypeStruct(*out[:2]) for out...  15.3 us
    all_to_all x1, blocking collectives, on_device(): sums = lax.all_to_all(sums, 'chan', 0, 0)  14.9 us
  transfers between devices with their start and end apart: 2, of which 2 were waited for; matrix products, arithmetic and copies ran while one was open for 0% of the time, Pallas kernels for 11%

profile of v4, /device:TPU:64, one launch (start us, length us, event | category | flops | bytes accessed | tf_op | source)
XLA Modules:
  0.0 65.7 jit_solution(6777117899846929387)
XLA Ops:
  0.6 0.0 copy-start.4
  0.6 0.0 copy-start.8
  0.7 0.0 copy-start.3
  0.7 2.6 %shard_map.121 = bf16[32,32,128]{2,1,0:T(8,128)(2,1)} custom-call(s32[256]{0:T(256)} %starts_ref.3, bf16[512,512]{1,0:T(8,128)(2,1)} %key_hbm.3, bf16[512,512]{1,0:T(8,128)(2,1)} %value_hbm.3, f32[8,512]{1,0:T(8,128)} %rate_hbm.1), custom_call_target="tpu_custom_call" | custom-call | flops 5242880 | bytes 655360 | tf_op jit(solution)/shard_map/pallas_call | solution.py:541
  3.2 0.0 copy-start.2
  3.2 12.7 %all-to-all-start = ((bf16[32,32,128]{2,1,0:T(8,128)(2,1)}), bf16[32,32,128]{2,1,0:T(8,128)(2,1)S(1)}, u32[]{:S(2)}, u32[]{:S(2)}) async-start(bf16[32,32,128]{2,1,0:T(8,128)(2,1)} %shard_map.121), calls=%async_computation | async-start | bytes 524288 | tf_op jit(solution)/shard_map/all_to_all | solution.py:598
  16.0 0.0 copy-done.4
  16.0 0.0 copy-done.8
  16.0 0.0 copy-start.7
  16.0 0.0 copy-start.6
  16.1 0.0 copy-start.5
  16.1 0.0 copy-done.3
  16.1 0.0 copy-done.2
  16.1 0.6 copy-done.7
  16.7 0.0 copy-done.6
  16.7 0.0 copy-done.5
  16.7 0.0 copy-start
  16.7 0.0 copy-start.1
  16.7 3.0 %shard_map.120 = (f32[4,512,128]{2,1,0:T(8,128)S(1)}, f32[136,128]{1,0:T(8,128)S(1)}) custom-call(s32[256]{0:T(256)S(1)} %copy-done.5, bf16[512,512]{1,0:T(8,128)(2,1)S(1)} %copy-done.2, bf16[512,512]{1,0:T(8,128)(2,1)S(1)} %copy-done.3, f32[8,512]{1,0:T(8,128)S(1)} %copy-done.4, f32[8,512]{1,0:T(8,128)S(1)} %sqrt_multiply_fusion.weight_ref, ...), custom_call_target="tpu_custom_call" | custom-call | flops 13107200 | bytes 1638400 | tf_op jit(solution)/shard_map/pallas_call | solution.py:541
  19.8 8.5 %all-to-all-done.got_ref = bf16[32,32,128]{2,1,0:T(8,128)(2,1)S(1)} async-done(((bf16[32,32,128]{2,1,0:T(8,128)(2,1)}), bf16[32,32,128]{2,1,0:T(8,128)(2,1)S(1)}, u32[]{:S(2)}, u32[]{:S(2)}) %all-to-all-start) | async-done | bytes 262176 | tf_op jit(solution)/shard_map/all_to_all | solution.py:598
  28.3 0.0 copy-done
  28.3 0.0 copy-done.1
  28.3 1.2 %shard_map.122 = (bf16[512,512]{1,0:T(8,128)(2,1)S(1)}, f32[16,8,128]{2,1,0:T(8,128)S(1)}) custom-call(f32[136,128]{1,0:T(8,128)S(1)} %get-tuple-element.19.table_ref, bf16[32,32,128]{2,1,0:T(8,128)(2,1)S(1)} %all-to-all-done.got_ref, f32[4,512,128]{2,1,0:T(8,128)S(1)} %get-tuple-element.20.conv_ref, bf16[512,512]{1,0:T(8,128)(2,1)S(1)} %copy-done, ...), custom_call_target="tpu_custom_call" | custom-call | flops 7864320 | bytes 983040 | tf_op jit(solution)/shard_map/pallas_call | solution.py:541
  29.4 14.9 %all_to_all.15.sums_ref = f32[16,8,128]{2,1,0:T(8,128)S(1)} all-to-all(f32[16,8,128]{2,1,0:T(8,128)S(1)} %get-tuple-element.21), channel_id=1, replica_groups=mesh['seq'=32,'chan'=16] {'chan'}, dimensions={0} | all-to-all | bytes 131072 | tf_op jit(solution)/shard_map/all_to_all | solution.py:613
  44.3 1.9 %shard_map.123 = (bf16[512,512]{1,0:T(8,128)(2,1)S(1)}, bf16[32,32,128]{2,1,0:T(8,128)(2,1)}, f32[8,128]{1,0:T(8,128)S(1)}) custom-call(f32[136,128]{1,0:T(8,128)S(1)} %get-tuple-element.19.table_ref, f32[16,8,128]{2,1,0:T(8,128)S(1)} %all_to_all.15.sums_ref, bf16[512,512]{1,0:T(8,128)(2,1)S(1)} %copy-done, bf16[512,512]{1,0:T(8,128)(2,1)S(1)} %copy-done.1, ...), custom_call_target="tpu_custom_call" | custom-call | flops 7864320 | bytes 983040 | tf_op jit(solution)/shard_map/pallas_call | solution.py:541
  46.2 4.6 %all-to-all-start.2 = ((bf16[32,32,128]{2,1,0:T(8,128)(2,1)}), bf16[32,32,128]{2,1,0:T(8,128)(2,1)S(1)}, u32[]{:S(2)}, u32[]{:S(2)}) async-start(bf16[32,32,128]{2,1,0:T(8,128)(2,1)} %get-tuple-element.29), calls=%async_computation.2 | async-start | bytes 524288 | tf_op jit(solution)/shard_map/all_to_all | solution.py:621
  50.8 1.5 %shard_map.124 = (bf16[512,512]{1,0:T(8,128)(2,1)}, bf16[512,512]{1,0:T(8,128)(2,1)}, f32[8,128]{1,0:T(8,128)S(1)}) custom-call(f32[136,128]{1,0:T(8,128)S(1)} %get-tuple-element.19.table_ref, f32[8,128]{1,0:T(8,128)S(1)} %get-tuple-element.23.totals_ref, bf16[512,512]{1,0:T(8,128)(2,1)S(1)} %copy-done, bf16[512,512]{1,0:T(8,128)(2,1)S(1)} %copy-done.1, ...), custom_call_target="tpu_custom_call" | custom-call | flops 5242880 | bytes 655360 | tf_op jit(solution)/shard_map/pallas_call | solution.py:541
  52.3 3.0 %shard_map.125 = (f32[2,512,128]{2,1,0:T(8,128)S(1)}, f32[2,512,128]{2,1,0:T(8,128)S(1)}, f32[64,128]{1,0:T(8,128)S(1)}) custom-call(s32[256]{0:T(256)S(1)} %copy-done.5, f32[136,128]{1,0:T(8,128)S(1)} %get-tuple-element.19.table_ref, bf16[512,512]{1,0:T(8,128)(2,1)S(1)} %get-tuple-element.26.adjoint_ref, f32[8,128]{1,0:T(8,128)S(1)} %get-tuple-element.27.done_ref), custom_call_target="tpu_custom_call" | custom-call | flops 13107200 | bytes 1638400 | tf_op jit(solution)/shard_map/pallas_call | solution.py:541
  55.3 8.3 %all-to-all-done.2.got_ref = bf16[32,32,128]{2,1,0:T(8,128)(2,1)S(1)} async-done(((bf16[32,32,128]{2,1,0:T(8,128)(2,1)}), bf16[32,32,128]{2,1,0:T(8,128)(2,1)S(1)}, u32[]{:S(2)}, u32[]{:S(2)}) %all-to-all-start.2) | async-done | bytes 262176 | tf_op jit(solution)/shard_map/all_to_all | solution.py:621
  63.6 2.1 %shard_map.126 = (bf16[512,512]{1,0:T(8,128)(2,1)}, bf16[512,512]{1,0:T(8,128)(2,1)}) custom-call(f32[136,128]{1,0:T(8,128)S(1)} %get-tuple-element.19.table_ref, f32[64,128]{1,0:T(8,128)S(1)} %get-tuple-element.28.flags_ref, bf16[32,32,128]{2,1,0:T(8,128)(2,1)S(1)} %all-to-all-done.2.got_ref, f32[2,512,128]{2,1,0:T(8,128)S(1)} %get-tuple-element.30.head_ref, ...), custom_call_target="tpu_custom_call" | custom-call | flops 7864320 | bytes 983040 | tf_op jit(solution)/shard_map/pallas_call | solution.py:541
  (1 shorter events, 0.0 us)
Async XLA Ops:
  0.6 15.3 %copy-start.4 = (f32[8,512]{1,0:T(8,128)S(1)}, f32[8,512]{1,0:T(8,128)}, u32[]{:S(2)}) copy-start(f32[8,512]{1,0:T(8,128)} %rate_hbm.1) | copy-start | bytes 49156
  0.6 15.3 %copy-start.8 = (f32[8,512]{1,0:T(8,128)S(1)}, f32[8,512]{1,0:T(8,128)}, u32[]{:S(2)}) copy-start(f32[8,512]{1,0:T(8,128)} %param.13) | copy-start | bytes 49156
  0.7 15.4 %copy-start.3 = (bf16[512,512]{1,0:T(8,128)(2,1)S(1)}, bf16[512,512]{1,0:T(8,128)(2,1)}, u32[]{:S(2)}) copy-start(bf16[512,512]{1,0:T(8,128)(2,1)} %value_hbm.3) | copy-start | bytes 1572868
  3.2 12.8 %copy-start.2 = (bf16[512,512]{1,0:T(8,128)(2,1)S(1)}, bf16[512,512]{1,0:T(8,128)(2,1)}, u32[]{:S(2)}) copy-start(bf16[512,512]{1,0:T(8,128)(2,1)} %key_hbm.3) | copy-start | bytes 1572868
  3.2 25.0 %all-to-all-start = ((bf16[32,32,128]{2,1,0:T(8,128)(2,1)}), bf16[32,32,128]{2,1,0:T(8,128)(2,1)S(1)}, u32[]{:S(2)}, u32[]{:S(2)}) async-start(bf16[32,32,128]{2,1,0:T(8,128)(2,1)} %shard_map.121), calls=%async_computation | async-start | bytes 524288 | tf_op jit(solution)/shard_map/all_to_all | solution.py:598
  16.0 0.7 %copy-start.7 = (f32[512]{0:T(512)S(1)}, f32[512]{0:T(512)}, u32[]{:S(2)}) copy-start(f32[512]{0:T(512)} %param.14) | copy-start | bytes 6148
  16.0 0.7 %copy-start.6 = (f32[512]{0:T(512)S(1)}, f32[512]{0:T(512)}, u32[]{:S(2)}) copy-start(f32[512]{0:T(512)} %param.15) | copy-start | bytes 6148
  16.1 0.7 %copy-start.5 = (s32[256]{0:T(256)S(1)}, s32[256]{0:T(256)}, u32[]{:S(2)}) copy-start(s32[256]{0:T(256)} %starts_ref.3) | copy-start | bytes 3076
  16.7 11.5 %copy-start = (bf16[512,512]{1,0:T(8,128)(2,1)S(1)}, bf16[512,512]{1,0:T(8,128)(2,1)}, u32[]{:S(2)}) copy-start(bf16[512,512]{1,0:T(8,128)(2,1)} %query_ref.5) | copy-start | bytes 1572868
  16.7 11.5 %copy-start.1 = (bf16[512,512]{1,0:T(8,128)(2,1)S(1)}, bf16[512,512]{1,0:T(8,128)(2,1)}, u32[]{:S(2)}) copy-start(bf16[512,512]{1,0:T(8,128)(2,1)} %cot_ref.5) | copy-start | bytes 1572868
  46.2 17.4 %all-to-all-start.2 = ((bf16[32,32,128]{2,1,0:T(8,128)(2,1)}), bf16[32,32,128]{2,1,0:T(8,128)(2,1)S(1)}, u32[]{:S(2)}, u32[]{:S(2)}) async-start(bf16[32,32,128]{2,1,0:T(8,128)(2,1)} %get-tuple-element.29), calls=%async_computation.2 | async-start | bytes 524288 | tf_op jit(solution)/shard_map/all_to_all | solution.py:621
